TPU v7x, 32 devices: a whole 2x2x4 slice. The times are simulated.
32 devices in a mesh: section: 2 (over x), dp: 8 (over z, y), rep: 2 (over core).
Axes of the slice: x: 2, y: 2, z: 4, core: 2. Of those that a mesh axis runs over, the one named last changes fastest.
Arguments:
- encoder_input: bfloat16 [32, 1024, 512], P(('dp', 'rep')), may hold values from -6 to 6
- action_targets: float32 [32, 100, 14], P(('dp', 'rep')), may hold values from -6 to 6
- arm_counts: int32 [32], P(('dp', 'rep')), may hold values from 1 to 2
- encoder_project: bfloat16 [512, 1536], replicated, may hold values from -0.25 to 0.25
- encoder_combine: bfloat16 [512, 512], replicated, may hold values from -6 to 6
- encoder_expand: bfloat16 [512, 3200], replicated, may hold values from -0.25 to 0.25
- encoder_reduce: bfloat16 [3200, 512], replicated, may hold values from -0.21875 to 0.21875
- encoder_gains: float32 [2, 512], replicated, may hold values from 0.1 to 1.9
- encoder_shifts: float32 [2, 512], replicated, may hold values from -3 to 3
- query_embed: bfloat16 [100, 512], replicated, may hold values from -6 to 6
- decoder_project: bfloat16 [512, 1536], replicated, may hold values from -0.25 to 0.25
- decoder_combine: bfloat16 [512, 512], replicated, may hold values from -1.5 to 1.5
- cross_query: bfloat16 [512, 512], replicated, may hold values from -0.25 to 0.25
- cross_memory: bfloat16 [512, 1024], replicated, may hold values from -0.25 to 0.25
- cross_combine: bfloat16 [512, 512], replicated, may hold values from -6 to 6
- decoder_expand: bfloat16 [512, 3200], replicated, may hold values from -0.25 to 0.25
- decoder_reduce: bfloat16 [3200, 512], replicated, may hold values from -0.21875 to 0.21875
- decoder_gains: float32 [3, 512], replicated, may hold values from 0.1 to 1.9
- decoder_shifts: float32 [3, 512], replicated, may hold values from -3 to 3
- action_head: bfloat16 [512, 14], replicated, may hold values from -0.5 to 0.5
Outputs:
- memory: bfloat16 [32, 1024, 512], P(('dp', 'rep'))
- slab_gradient: bfloat16 [2, 32, 1024, 512], P('section', ('dp', 'rep'))
- grad_encoder_project: float32 [512, 1536], P(('section', 'dp'))
- grad_encoder_combine: float32 [512, 512], P(('section', 'dp'))
- grad_encoder_expand: float32 [512, 3200], P(('section', 'dp'))
- grad_encoder_reduce: float32 [3200, 512], P(('section', 'dp'))
- grad_encoder_gains: float32 [2, 512], P(None, ('section', 'dp'))
- grad_encoder_shifts: float32 [2, 512], P(None, ('section', 'dp'))
- grad_query_embed: float32 [100, 512], P(None, ('section', 'dp'))
- grad_decoder_project: float32 [512, 1536], P(('section', 'dp'))
- grad_decoder_combine: float32 [512, 512], P(('section', 'dp'))
- grad_cross_query: float32 [512, 512], P(('section', 'dp'))
- grad_cross_memory: float32 [512, 1024], P(('section', 'dp'))
- grad_cross_combine: float32 [512, 512], P(('section', 'dp'))
- grad_decoder_expand: float32 [512, 3200], P(('section', 'dp'))
- grad_decoder_reduce: float32 [3200, 512], P(('section', 'dp'))
- grad_decoder_gains: float32 [3, 512], P(None, ('section', 'dp'))
- grad_decoder_shifts: float32 [3, 512], P(None, ('section', 'dp'))
- grad_action_head: float32 [512, 14], P(('section', 'dp'))
All inputs are finite; a program needn't handle non-finite values.
Results may differ from a plain program's by a relative error of at most 0.012.
Values may be sent and summed in bfloat16 or wider, within the bound.
A program may use at most 320 MiB of HBM per device.

v0:
```python
import jax
import jax.numpy as jnp
from jax import lax
from jax.sharding import PartitionSpec as P

HEADS = 8


EPSILON = 1e-05


def from_behind(array, axis, by):
    count = lax.axis_size(axis)
    pairs = [(i, i + by) for i in range(count) if 0 <= i + by < count]
    return lax.ppermute(array, axis, pairs)


def from_partner(value, axis, bit):
    mask = 2**bit
    pairs = [(source, source ^ mask) for source in range(lax.axis_size(axis))]
    return lax.ppermute(value, axis, pairs)


def product(left_side, right_side):
    return jnp.dot(left_side, right_side, preferred_element_type=jnp.float32)


def product_left(left_side, right_side):
    return lax.dot_general(
        left_side, right_side, (((0,), (0,)), ((), ())), preferred_element_type=jnp.float32
    )


def product_right(left_side, right_side):
    return lax.dot_general(
        left_side, right_side, (((1,), (1,)), ((), ())), preferred_element_type=jnp.float32
    )


def layer_norm(residual, gain_row, shift_row):
    centre = jnp.mean(residual, axis=-1, keepdims=True)
    centred = residual - centre
    spread = jnp.mean(centred * centred, axis=-1, keepdims=True)
    return centred * lax.rsqrt(spread + EPSILON) * gain_row + shift_row


def gelu_tanh(values):
    return jax.nn.gelu(values, approximate=True)


def split_heads(matrix):
    return matrix.reshape(matrix.shape[0], HEADS, matrix.shape[1] // HEADS)


def attend_forward(queries, key_rows, value_rows):
    row_count = queries.shape[0]
    block_rows = min(512, row_count)
    score_scale = (queries.shape[1] // HEADS) ** (-0.5)
    key_heads = split_heads(key_rows)
    value_heads = split_heads(value_rows)
    query_blocks = split_heads(queries).reshape(row_count // block_rows, block_rows, HEADS, -1)

    def one_block(query_heads):
        scores = (
            jnp.einsum("qhd,khd->hqk", query_heads, key_heads, preferred_element_type=jnp.float32)
            * score_scale
        )
        largest = jnp.max(scores, axis=-1, keepdims=True)
        raised = jnp.exp(scores - largest)
        row_total = jnp.sum(raised, axis=-1, keepdims=True)
        weights = (raised / row_total).astype(jnp.bfloat16)
        mixed_heads = jnp.einsum(
            "hqk,khd->qhd", weights, value_heads, preferred_element_type=jnp.float32
        )
        return (mixed_heads.astype(jnp.bfloat16), (largest + jnp.log(row_total))[:, :, 0])

    mixed_blocks, log_totals = lax.map(one_block, query_blocks)
    return (mixed_blocks.reshape(row_count, queries.shape[1]), log_totals)


def attend_backward(queries, key_rows, value_rows, log_totals, grad_mixed):
    row_count = queries.shape[0]
    column_count = key_rows.shape[0]
    model_width = queries.shape[1]
    block_rows = min(512, row_count)
    score_scale = (model_width // HEADS) ** (-0.5)
    key_heads = split_heads(key_rows)
    value_heads = split_heads(value_rows)
    query_blocks = split_heads(queries).reshape(row_count // block_rows, block_rows, HEADS, -1)
    grad_blocks = split_heads(grad_mixed).reshape(row_count // block_rows, block_rows, HEADS, -1)

    def one_block(pieces):
        query_heads, log_block, grad_heads = pieces
        scores = (
            jnp.einsum("qhd,khd->hqk", query_heads, key_heads, preferred_element_type=jnp.float32)
            * score_scale
        )
        probs = jnp.exp(scores - log_block[:, :, None])
        rounded = probs.astype(jnp.bfloat16)
        grad_values = jnp.einsum(
            "hqk,qhd->khd", rounded, grad_heads, preferred_element_type=jnp.float32
        )
        grad_probs = jnp.einsum(
            "qhd,khd->hqk", grad_heads, value_heads, preferred_element_type=jnp.float32
        )
        inner_sum = jnp.sum(probs * grad_probs, axis=-1, keepdims=True)
        grad_scores = (probs * (grad_probs - inner_sum)).astype(jnp.bfloat16)
        grad_queries = (
            jnp.einsum("hqk,khd->qhd", grad_scores, key_heads, preferred_element_type=jnp.float32)
            * score_scale
        )
        grad_keys = (
            jnp.einsum("hqk,qhd->khd", grad_scores, query_heads, preferred_element_type=jnp.float32)
            * score_scale
        )
        return (grad_queries, grad_keys, grad_values)

    grad_queries, grad_keys, grad_values = lax.map(
        one_block, (query_blocks, log_totals, grad_blocks)
    )
    return (
        grad_queries.reshape(row_count, model_width),
        jnp.sum(grad_keys, axis=0).reshape(column_count, model_width),
        jnp.sum(grad_values, axis=0).reshape(column_count, model_width),
    )


def episode_loss(predicted, target, arm_count):
    misfit = predicted - target
    joint_index = lax.broadcasted_iota(jnp.int32, predicted.shape, 1)
    active = (joint_index < predicted.shape[1] // 2 * arm_count).astype(jnp.float32)
    return (
        2.0
        / arm_count.astype(jnp.float32)
        * jnp.sum(active * (jnp.sqrt(misfit * misfit + 1.0) - 1.0))
    )


def encoder_forward(inputs, weights):
    project_w, combine_w, expand_w, reduce_w, gain_rows, shift_rows = weights
    model_width = inputs.shape[1]
    packed = product(inputs, project_w).astype(jnp.bfloat16)
    mixed_heads, log_totals = attend_forward(
        packed[:, :model_width],
        packed[:, model_width : 2 * model_width],
        packed[:, 2 * model_width :],
    )
    first_resid = inputs.astype(jnp.float32) + product(mixed_heads, combine_w)
    first_norm = layer_norm(first_resid, gain_rows[0], shift_rows[0])
    first_low = first_norm.astype(jnp.bfloat16)
    hidden = product(first_low, expand_w)
    activated = gelu_tanh(hidden).astype(jnp.bfloat16)
    second_resid = first_norm + product(activated, reduce_w)
    layer_out = layer_norm(second_resid, gain_rows[1], shift_rows[1])
    return (
        layer_out,
        (packed, mixed_heads, log_totals, first_resid, first_low, hidden, activated, second_resid),
    )


def encoder_backward(inputs, grad_layer, weights):
    project_w, combine_w, expand_w, reduce_w, gain_rows, shift_rows = weights
    model_width = inputs.shape[1]
    unused, saved = encoder_forward(inputs, weights)
    packed, mixed_heads, log_totals, first_resid, first_low, hidden, activated, second_resid = saved
    unused, norm_later = jax.vjp(layer_norm, second_resid, gain_rows[1], shift_rows[1])
    grad_second, grad_gain_later, grad_shift_later = norm_later(grad_layer)
    grad_branch = grad_second.astype(jnp.bfloat16)
    grad_reduce = product_left(activated, grad_branch)
    unused, gelu_back = jax.vjp(gelu_tanh, hidden)
    grad_hidden = gelu_back(product_right(grad_branch, reduce_w))[0].astype(jnp.bfloat16)
    grad_expand = product_left(first_low, grad_hidden)
    grad_first = grad_second + product_right(grad_hidden, expand_w)
    unused, norm_earlier = jax.vjp(layer_norm, first_resid, gain_rows[0], shift_rows[0])
    grad_first_resid, grad_gain_earlier, grad_shift_earlier = norm_earlier(grad_first)
    grad_attn_branch = grad_first_resid.astype(jnp.bfloat16)
    grad_combine = product_left(mixed_heads, grad_attn_branch)
    grad_mixed = product_right(grad_attn_branch, combine_w).astype(jnp.bfloat16)
    grad_queries, grad_keys, grad_values = attend_backward(
        packed[:, :model_width],
        packed[:, model_width : 2 * model_width],
        packed[:, 2 * model_width :],
        log_totals,
        grad_mixed,
    )
    grad_packed = jnp.concatenate([grad_queries, grad_keys, grad_values], axis=1).astype(
        jnp.bfloat16
    )
    grad_project = product_left(inputs, grad_packed)
    grad_inputs = grad_first_resid + product_right(grad_packed, project_w)
    return (
        grad_inputs.astype(jnp.bfloat16),
        (
            grad_project,
            grad_combine,
            grad_expand,
            grad_reduce,
            jnp.stack([grad_gain_earlier, grad_gain_later]),
            jnp.stack([grad_shift_earlier, grad_shift_later]),
        ),
    )


def decoder_step(memory_rows, target, arm_count, weights):
    (
        starts,
        project_w,
        combine_w,
        query_w,
        memory_w,
        cross_w,
        expand_w,
        reduce_w,
        gain_rows,
        shift_rows,
        head_w,
    ) = weights
    model_width = starts.shape[1]
    packed = product(starts, project_w).astype(jnp.bfloat16)
    self_mixed, self_logs = attend_forward(
        packed[:, :model_width],
        packed[:, model_width : 2 * model_width],
        packed[:, 2 * model_width :],
    )
    first_resid = starts.astype(jnp.float32) + product(self_mixed, combine_w)
    first_norm = layer_norm(first_resid, gain_rows[0], shift_rows[0])
    first_low = first_norm.astype(jnp.bfloat16)
    cross_queries = product(first_low, query_w).astype(jnp.bfloat16)
    memory_pair = product(memory_rows, memory_w).astype(jnp.bfloat16)
    cross_mixed, cross_logs = attend_forward(
        cross_queries, memory_pair[:, :model_width], memory_pair[:, model_width:]
    )
    second_resid = first_norm + product(cross_mixed, cross_w)
    second_norm = layer_norm(second_resid, gain_rows[1], shift_rows[1])
    second_low = second_norm.astype(jnp.bfloat16)
    hidden = product(second_low, expand_w)
    activated = gelu_tanh(hidden).astype(jnp.bfloat16)
    third_resid = second_norm + product(activated, reduce_w)
    third_norm = layer_norm(third_resid, gain_rows[2], shift_rows[2])
    third_low = third_norm.astype(jnp.bfloat16)
    predicted = product(third_low, head_w)
    unused, loss_back = jax.vjp(lambda guess: episode_loss(guess, target, arm_count), predicted)
    grad_predicted = loss_back(jnp.ones((), jnp.float32))[0].astype(jnp.bfloat16)
    grad_head = product_left(third_low, grad_predicted)
    grad_third = product_right(grad_predicted, head_w)
    unused, norm_third = jax.vjp(layer_norm, third_resid, gain_rows[2], shift_rows[2])
    grad_third_resid, grad_gain_third, grad_shift_third = norm_third(grad_third)
    grad_branch = grad_third_resid.astype(jnp.bfloat16)
    grad_reduce = product_left(activated, grad_branch)
    unused, gelu_back = jax.vjp(gelu_tanh, hidden)
    grad_hidden = gelu_back(product_right(grad_branch, reduce_w))[0].astype(jnp.bfloat16)
    grad_expand = product_left(second_low, grad_hidden)
    grad_second = grad_third_resid + product_right(grad_hidden, expand_w)
    unused, norm_second = jax.vjp(layer_norm, second_resid, gain_rows[1], shift_rows[1])
    grad_second_resid, grad_gain_second, grad_shift_second = norm_second(grad_second)
    grad_cross_branch = grad_second_resid.astype(jnp.bfloat16)
    grad_cross_w = product_left(cross_mixed, grad_cross_branch)
    grad_cross_mixed = product_right(grad_cross_branch, cross_w).astype(jnp.bfloat16)
    grad_cross_queries, grad_keys, grad_values = attend_backward(
        cross_queries,
        memory_pair[:, :model_width],
        memory_pair[:, model_width:],
        cross_logs,
        grad_cross_mixed,
    )
    grad_pair = jnp.concatenate([grad_keys, grad_values], axis=1).astype(jnp.bfloat16)
    grad_memory_w = product_left(memory_rows, grad_pair)
    grad_memory = product_right(grad_pair, memory_w).astype(jnp.bfloat16)
    grad_query_low = grad_cross_queries.astype(jnp.bfloat16)
    grad_query_w = product_left(first_low, grad_query_low)
    grad_first = grad_second_resid + product_right(grad_query_low, query_w)
    unused, norm_first = jax.vjp(layer_norm, first_resid, gain_rows[0], shift_rows[0])
    grad_first_resid, grad_gain_first, grad_shift_first = norm_first(grad_first)
    grad_self_branch = grad_first_resid.astype(jnp.bfloat16)
    grad_combine = product_left(self_mixed, grad_self_branch)
    grad_self_mixed = product_right(grad_self_branch, combine_w).astype(jnp.bfloat16)
    grad_self_queries, grad_self_keys, grad_self_values = attend_backward(
        packed[:, :model_width],
        packed[:, model_width : 2 * model_width],
        packed[:, 2 * model_width :],
        self_logs,
        grad_self_mixed,
    )
    grad_packed = jnp.concatenate(
        [grad_self_queries, grad_self_keys, grad_self_values], axis=1
    ).astype(jnp.bfloat16)
    grad_project = product_left(starts, grad_packed)
    grad_starts = grad_first_resid + product_right(grad_packed, project_w)
    grad_gains = jnp.stack([grad_gain_first, grad_gain_second, grad_gain_third])
    grad_shifts = jnp.stack([grad_shift_first, grad_shift_second, grad_shift_third])
    return (
        grad_memory,
        (
            grad_starts,
            grad_project,
            grad_combine,
            grad_query_w,
            grad_memory_w,
            grad_cross_w,
            grad_expand,
            grad_reduce,
            grad_gains,
            grad_shifts,
            grad_head,
        ),
    )


def per_device(
    encoder_input,
    action_targets,
    arm_counts,
    encoder_project,
    encoder_combine,
    encoder_expand,
    encoder_reduce,
    encoder_gains,
    encoder_shifts,
    query_embed,
    decoder_project,
    decoder_combine,
    cross_query,
    cross_memory,
    cross_combine,
    decoder_expand,
    decoder_reduce,
    decoder_gains,
    decoder_shifts,
    action_head,
):
    on_encoder = lax.axis_index("section") == 0
    encoder_weights = (
        encoder_project,
        encoder_combine,
        encoder_expand,
        encoder_reduce,
        encoder_gains,
        encoder_shifts,
    )
    decoder_weights = (
        query_embed,
        decoder_project,
        decoder_combine,
        cross_query,
        cross_memory,
        cross_combine,
        decoder_expand,
        decoder_reduce,
        decoder_gains,
        decoder_shifts,
        action_head,
    )
    empty_rows = jnp.zeros(encoder_input.shape[1:], jnp.bfloat16)
    encoder_zeros = tuple((jnp.zeros(item.shape, jnp.float32) for item in encoder_weights))
    decoder_zeros = tuple((jnp.zeros(item.shape, jnp.float32) for item in decoder_weights))

    def forward_turn(carried, inputs):
        layer_rows = lax.cond(
            on_encoder,
            lambda: encoder_forward(inputs, encoder_weights)[0].astype(jnp.bfloat16),
            lambda: empty_rows,
        )
        arrived = from_behind(layer_rows, "section", 1)
        return (carried, (layer_rows, arrived))

    unused, (sent_rows, arrived_rows) = lax.scan(
        forward_turn, jnp.zeros((), jnp.int32), encoder_input
    )

    def decoder_turn(totals, pieces):
        memory_rows, target, arm_count = pieces
        grad_memory, fresh = lax.cond(
            on_encoder,
            lambda: (empty_rows, decoder_zeros),
            lambda: decoder_step(memory_rows, target, arm_count, decoder_weights),
        )
        returned = from_behind(grad_memory, "section", -1)
        return (tuple((old + new for old, new in zip(totals, fresh))), (grad_memory, returned))

    decoder_totals, (memory_grads, returned_rows) = lax.scan(
        decoder_turn, decoder_zeros, (arrived_rows, action_targets, arm_counts)
    )

    def encoder_turn(totals, pieces):
        inputs, grad_layer = pieces
        grad_inputs, fresh = lax.cond(
            on_encoder,
            lambda: encoder_backward(inputs, grad_layer.astype(jnp.float32), encoder_weights),
            lambda: (empty_rows, encoder_zeros),
        )
        return (tuple((old + new for old, new in zip(totals, fresh))), grad_inputs)

    encoder_totals, input_grads = lax.scan(
        encoder_turn, encoder_zeros, (encoder_input, returned_rows)
    )
    memory_out = jnp.where(on_encoder, sent_rows, arrived_rows)
    slab_out = jnp.where(on_encoder, input_grads, memory_grads)[None]
    decoder_main = (decoder_totals[1], decoder_totals[2], decoder_totals[6], decoder_totals[7])
    lane_count = lax.axis_size("dp")
    pairs = list(zip(encoder_totals[:4], decoder_main)) + [
        (decoder_totals[3], decoder_totals[3]),
        (decoder_totals[4], decoder_totals[4]),
        (decoder_totals[5], decoder_totals[5]),
    ]
    own_parts = [
        jnp.where(on_encoder, encoder_part, decoder_part).reshape(
            2, lane_count, encoder_part.shape[0] // (2 * lane_count), encoder_part.shape[1]
        )
        for encoder_part, decoder_part in pairs
    ]
    summed = (
        lax.psum_scatter(own_parts[0], "dp", scatter_dimension=1, tiled=True),
        lax.psum_scatter(own_parts[1], "dp", scatter_dimension=1, tiled=True),
        lax.psum_scatter(own_parts[2], "dp", scatter_dimension=1, tiled=True),
        lax.psum_scatter(own_parts[3], "dp", scatter_dimension=1, tiled=True),
        lax.psum_scatter(own_parts[4], "dp", scatter_dimension=1, tiled=True),
        lax.psum_scatter(own_parts[5], "dp", scatter_dimension=1, tiled=True),
        lax.psum_scatter(own_parts[6], "dp", scatter_dimension=1, tiled=True),
    )
    kept_parts = [jnp.where(on_encoder, item[0, 0], item[1, 0]) for item in summed]
    leaving = [jnp.where(on_encoder, item[1, 0], item[0, 0]) for item in summed]
    arrived_parts = (
        from_partner(leaving[0].astype(jnp.bfloat16), "section", 0).astype(jnp.float32),
        from_partner(leaving[1].astype(jnp.bfloat16), "section", 0).astype(jnp.float32),
        from_partner(leaving[2].astype(jnp.bfloat16), "section", 0).astype(jnp.float32),
        from_partner(leaving[3].astype(jnp.bfloat16), "section", 0).astype(jnp.float32),
        from_partner(leaving[4].astype(jnp.bfloat16), "section", 0).astype(jnp.float32),
        from_partner(leaving[5].astype(jnp.bfloat16), "section", 0).astype(jnp.float32),
        from_partner(leaving[6].astype(jnp.bfloat16), "section", 0).astype(jnp.float32),
    )
    encoder_common = tuple(
        (
            jnp.where(on_encoder, mine, theirs)
            for mine, theirs in zip(kept_parts[:4], arrived_parts[:4])
        )
    )
    decoder_common = tuple(
        (
            jnp.where(on_encoder, theirs, mine)
            for mine, theirs in zip(kept_parts[:4], arrived_parts[:4])
        )
    )
    cross_common = tuple(
        (
            jnp.where(on_encoder, theirs, mine)
            for mine, theirs in zip(kept_parts[4:], arrived_parts[4:])
        )
    )
    small = (
        lax.psum_scatter(encoder_totals[4], ("section", "dp"), scatter_dimension=1, tiled=True),
        lax.psum_scatter(encoder_totals[5], ("section", "dp"), scatter_dimension=1, tiled=True),
        lax.psum_scatter(decoder_totals[0], ("section", "dp"), scatter_dimension=1, tiled=True),
        lax.psum_scatter(decoder_totals[8], ("section", "dp"), scatter_dimension=1, tiled=True),
        lax.psum_scatter(decoder_totals[9], ("section", "dp"), scatter_dimension=1, tiled=True),
        lax.psum_scatter(decoder_totals[10], ("section", "dp"), scatter_dimension=0, tiled=True),
    )
    encoder_norms = (small[0], small[1])
    query_sum = small[2]
    decoder_norms = (small[3], small[4])
    head_sum = small[5]
    summed_all = (
        lax.psum(encoder_common[0].astype(jnp.bfloat16), "rep").astype(jnp.float32),
        lax.psum(encoder_common[1].astype(jnp.bfloat16), "rep").astype(jnp.float32),
        lax.psum(encoder_common[2].astype(jnp.bfloat16), "rep").astype(jnp.float32),
        lax.psum(encoder_common[3].astype(jnp.bfloat16), "rep").astype(jnp.float32),
        lax.psum(encoder_norms[0].astype(jnp.bfloat16), "rep").astype(jnp.float32),
        lax.psum(encoder_norms[1].astype(jnp.bfloat16), "rep").astype(jnp.float32),
        lax.psum(query_sum.astype(jnp.bfloat16), "rep").astype(jnp.float32),
        lax.psum(decoder_common[0].astype(jnp.bfloat16), "rep").astype(jnp.float32),
        lax.psum(decoder_common[1].astype(jnp.bfloat16), "rep").astype(jnp.float32),
        lax.psum(cross_common[0].astype(jnp.bfloat16), "rep").astype(jnp.float32),
        lax.psum(cross_common[1].astype(jnp.bfloat16), "rep").astype(jnp.float32),
        lax.psum(cross_common[2].astype(jnp.bfloat16), "rep").astype(jnp.float32),
        lax.psum(decoder_common[2].astype(jnp.bfloat16), "rep").astype(jnp.float32),
        lax.psum(decoder_common[3].astype(jnp.bfloat16), "rep").astype(jnp.float32),
        lax.psum(decoder_norms[0].astype(jnp.bfloat16), "rep").astype(jnp.float32),
        lax.psum(decoder_norms[1].astype(jnp.bfloat16), "rep").astype(jnp.float32),
        lax.psum(head_sum.astype(jnp.bfloat16), "rep").astype(jnp.float32),
    )
    return (memory_out, slab_out) + tuple(summed_all)


def solution(mesh):
    placed = (
        P(("dp", "rep"), None, None),
        P(("dp", "rep"), None, None),
        P(("dp", "rep")),
        P(),
        P(),
        P(),
        P(),
        P(),
        P(),
        P(),
        P(),
        P(),
        P(),
        P(),
        P(),
        P(),
        P(),
        P(),
        P(),
        P(),
    )
    return jax.shard_map(
        per_device,
        mesh=mesh,
        in_specs=placed,
        out_specs=(
            P(("dp", "rep"), None, None),
            P("section", ("dp", "rep"), None, None),
            P(("section", "dp"), None),
            P(("section", "dp"), None),
            P(("section", "dp"), None),
            P(("section", "dp"), None),
            P(None, ("section", "dp")),
            P(None, ("section", "dp")),
            P(None, ("section", "dp")),
            P(("section", "dp"), None),
            P(("section", "dp"), None),
            P(("section", "dp"), None),
            P(("section", "dp"), None),
            P(("section", "dp"), None),
            P(("section", "dp"), None),
            P(("section", "dp"), None),
            P(None, ("section", "dp")),
            P(None, ("section", "dp")),
            P(("section", "dp"), None),
        ),
        check_vma=False,
    )
```

profile of v0, /device:TPU:0, one launch (start us, length us, event | category | flops | bytes accessed | tf_op | source)
XLA Modules:
  0.0 2207.0 jit_solution(12243544692069419196)
XLA Ops:
  15.6 198.6 %while.149 = (s32[]{:T(128)}, bf16[2,1024,512]{2,1,0:T(8,128)(2,1)}, bf16[2,1024,512]{2,1,0:T(8,128)(2,1)}, pred[]{:T(512)}, bf16[2,1024,512]{1,2,0:T(8,128)(2,1...) while((s32[]{:T(128)}, bf16[2,1024,512]{2,1,0:T(8,128)(2,1)}, ...), condition=%wide.region_11.12_spmd, body=%wide.region_0.11_spmd.sunk | while | flops 10000141312 | bytes 123090960 | solution.py:366
  15.6 73.1 %conditional.8 = (bf16[1024,512]{0,1:T(8,128)(2,1)}, bf16[1,1024,512]{1,2,0:T(8,128)(2,1)}) conditional(s32[]{:T(128)} %convert_element_type.701, () %tuple.229, (bf16[2,1024,512]{1,2,0:T(8,128)(2,1)}, s32[]{:T(128)}, bf16[512,1536]{1,0:T(8,128)(2,1)}, bf16[512,512]{1,0:T(8,128)(2,1)}, f32[2,512]{1,0:T(2,128)}, /*index=5*/f32[2,512]{1,0:T(2,128)}, ...), branch_computations={%region_1.1_spmd, %region_2.10_spmd} | conditional | flops 10000141312 | bytes 110506792 | solution.py:358
  25.4 38.0 %while.148 = (s32[]{:T(128)}, bf16[2,512,8,64]{1,3,2,0:T(8,128)(2,1)}, bf16[2,512,8,64]{1,3,2,0:T(8,128)(2,1)S(1)}, bf16[1024,8,64]{0,2,1:T(8,128)(2,1)}, bf16[1024,8,64]{0,2,1:T(8,128)(2,1)}, /*index=5*/s32[]{:T(128)}) while((s32[]{:T(128)}, bf16[2,512,8,64]{1,3,2,0:T(8,128)(2,1)}, bf16[2,512,8,64]{1,3,2,0:T(8,128)(2,1)S(1)}, ...), condition=%wide.region_6.5_spmd, body=%wide.region_3.4_spmd.sunk | while | flops 1094976512 | bytes 49316008 | solution.py:77
  92.6 21.0 collective-permute-done.1
  115.2 73.1 %conditional.8 = (bf16[1024,512]{0,1:T(8,128)(2,1)}, bf16[1,1024,512]{1,2,0:T(8,128)(2,1)}) conditional(s32[]{:T(128)} %convert_element_type.701, () %tuple.229, (bf16[2,1024,512]{1,2,0:T(8,128)(2,1)}, s32[]{:T(128)}, bf16[512,1536]{1,0:T(8,128)(2,1)}, bf16[512,512]{1,0:T(8,128)(2,1)}, f32[2,512]{1,0:T(2,128)}, /*index=5*/f32[2,512]{1,0:T(2,128)}, ...), branch_computations={%region_1.1_spmd, %region_2.10_spmd} | conditional | flops 10000141312 | bytes 110506792 | solution.py:358
  125.0 38.0 %while.148 = (s32[]{:T(128)}, bf16[2,512,8,64]{1,3,2,0:T(8,128)(2,1)}, bf16[2,512,8,64]{1,3,2,0:T(8,128)(2,1)S(1)}, bf16[1024,8,64]{0,2,1:T(8,128)(2,1)}, bf16[1024,8,64]{0,2,1:T(8,128)(2,1)}, /*index=5*/s32[]{:T(128)}) while((s32[]{:T(128)}, bf16[2,512,8,64]{1,3,2,0:T(8,128)(2,1)}, bf16[2,512,8,64]{1,3,2,0:T(8,128)(2,1)S(1)}, ...), condition=%wide.region_6.5_spmd, body=%wide.region_3.4_spmd.sunk | while | flops 1094976512 | bytes 49316008 | solution.py:77
  168.9 16.4 fusion.209
  192.2 20.4 collective-permute-done.1
  215.6 219.9 %while.150 = (s32[]{:T(128)}, f32[100,512]{1,0:T(8,128)}, f32[512,1536]{0,1:T(8,128)}, f32[512,512]{1,0:T(8,128)}, f32[512,512]{1,0:T(8,128)}, /*index=5*/f32[51...) while((s32[]{:T(128)}, f32[100,512]{1,0:T(8,128)}, ...), condition=%wide.region_39.40_spmd.clone, body=%wide.region_12.39_spmd.clone.sunk | while | flops 6887316992 | bytes 445153280 | solution.py:380
  281.2 48.1 %collective-permute-done = bf16[1024,512]{1,0:T(8,128)(2,1)} collective-permute-done((bf16[1024,512]{1,0:T(8,128)(2,1)}, bf16[1024,512]{1,0:T(8,128)(2,1)}, u32[]{:S(2)}, u32[]{:S(2)}) %collective-permute-start) | collective-permute-done | bytes 1048608 | tf_op jit(solution)/shard_map/while/body/eval_jaxpr/ppermute | solution.py:15
  379.8 52.7 %collective-permute-done = bf16[1024,512]{1,0:T(8,128)(2,1)} collective-permute-done((bf16[1024,512]{1,0:T(8,128)(2,1)}, bf16[1024,512]{1,0:T(8,128)(2,1)}, u32[]{:S(2)}, u32[]{:S(2)}) %collective-permute-start) | collective-permute-done | bytes 1048608 | tf_op jit(solution)/shard_map/while/body/eval_jaxpr/ppermute | solution.py:15
  437.0 481.7 %while.151 = (s32[]{:T(128)}, f32[512,1536]{1,0:T(8,128)}, f32[512,512]{1,0:T(8,128)}, f32[512,3200]{1,0:T(8,128)}, f32[3200,512]{1,0:T(8,128)}, /*index=5*/f32[...) while((s32[]{:T(128)}, f32[512,1536]{1,0:T(8,128)}, ...), condition=%wide.region_64.65_spmd.clone, body=%wide.region_40.64_spmd.clone.sunk | while | flops 30625245184 | bytes 667593472 | solution.py:393
  443.8 208.2 %conditional.10 = (f32[512,1536]{1,0:T(8,128)}, f32[512,512]{1,0:T(8,128)}, f32[512,3200]{1,0:T(8,128)}, f32[3200,512]{1,0:T(8,128)}, f32[2,512]{1,0:T(2,128)}, ...) conditional(s32[]{:T(128)} %convert_element_type.703, () %tuple.238, (bf16[2,1024,512]{1,2,0:T(8,128)(2,1)}, ...), branch_computations={%region_41.41_spmd, %region_42.63_spmd} | conditional | flops 30616590336 | bytes 557139968 | solution.py:386
  460.7 22.8 %while.146 = (s32[]{:T(128)}, bf16[2,512,8,64]{1,3,2,0:T(8,128)(2,1)}, f32[2,8,512]{2,1,0:T(8,128)S(1)}, bf16[2,512,8,64]{1,3,2,0:T(8,128)(2,1)S(1)}, bf16[1024,...) while((s32[]{:T(128)}, bf16[2,512,8,64]{1,3,2,0:T(8,128)(2,1)}, ...), condition=%wide.region_46.45_spmd, body=%wide.region_43.44_spmd.sunk | while | flops 1111748608 | bytes 66191540 | solution.py:77
  562.1 73.4 %while.147 = (s32[]{:T(128)}, bf16[2,512,8,64]{1,3,2,0:T(8,128)(2,1)}, f32[2,1024,8,64]{1,3,2,0:T(8,128)}, f32[2,1024,8,64]{1,3,2,0:T(8,128)}, bf16[2,512,8,64]{...) while((s32[]{:T(128)}, ...), condition=%wide.region_57.56_spmd, body=%wide.region_55.55_spmd.sunk | while | flops 2735468544 | bytes 174180544 | solution.py:118
  676.9 208.1 %conditional.10 = (f32[512,1536]{1,0:T(8,128)}, f32[512,512]{1,0:T(8,128)}, f32[512,3200]{1,0:T(8,128)}, f32[3200,512]{1,0:T(8,128)}, f32[2,512]{1,0:T(2,128)}, ...) conditional(s32[]{:T(128)} %convert_element_type.703, () %tuple.238, (bf16[2,1024,512]{1,2,0:T(8,128)(2,1)}, ...), branch_computations={%region_41.41_spmd, %region_42.63_spmd} | conditional | flops 30616590336 | bytes 557139968 | solution.py:386
  693.7 22.8 %while.146 = (s32[]{:T(128)}, bf16[2,512,8,64]{1,3,2,0:T(8,128)(2,1)}, f32[2,8,512]{2,1,0:T(8,128)S(1)}, bf16[2,512,8,64]{1,3,2,0:T(8,128)(2,1)S(1)}, bf16[1024,...) while((s32[]{:T(128)}, bf16[2,512,8,64]{1,3,2,0:T(8,128)(2,1)}, ...), condition=%wide.region_46.45_spmd, body=%wide.region_43.44_spmd.sunk | while | flops 1111748608 | bytes 66191540 | solution.py:77
  795.2 73.4 %while.147 = (s32[]{:T(128)}, bf16[2,512,8,64]{1,3,2,0:T(8,128)(2,1)}, f32[2,1024,8,64]{1,3,2,0:T(8,128)}, f32[2,1024,8,64]{1,3,2,0:T(8,128)}, bf16[2,512,8,64]{...) while((s32[]{:T(128)}, ...), condition=%wide.region_57.56_spmd, body=%wide.region_55.55_spmd.sunk | while | flops 2735468544 | bytes 174180544 | solution.py:118
  940.5 824.2 %all-reduce.17 = (bf16[2,8,32,1536]{3,2,1,0:T(8,128)(2,1)}, bf16[2,8,32,512]{3,2,1,0:T(8,128)(2,1)}, bf16[2,8,32,3200]{3,2,1,0:T(8,128)(2,1)}, bf16[2,8,200,512]...) all-reduce(f32[2,8,32,1536]{3,2,1,0:T(8,128)} %bitcast.474, ...), channel_id=2, replica_groups=mesh['section'=2,'dp'=8,'rep'=2] {'dp'}, use_global_device_ids=true, to_apply=%region_65.66.clone | all-reduce | flops 5373952 | bytes 32243712
  1789.2 54.9 %reduce-scatter.40.cloned.1.call-done = f32[32,2]{1,0:T(8,128)} async-done(((f32[512,2]{1,0:T(8,128)}), f32[32,2]{1,0:T(8,128)}) %reduce-scatter.40.cloned.1.call-update) | async-done | bytes 272
  1845.4 74.1 %reduce-scatter.42.cloned.1.call-done = f32[32,3]{1,0:T(8,128)} async-done(((f32[512,3]{1,0:T(8,128)}), f32[32,3]{1,0:T(8,128)}) %reduce-scatter.42.cloned.1.call-update) | async-done | bytes 400
  1920.9 73.5 %reduce-scatter.44.cloned.1.call-done = f32[32,3]{1,0:T(8,128)} async-done(((f32[512,3]{1,0:T(8,128)}), f32[32,3]{1,0:T(8,128)}) %reduce-scatter.44.cloned.1.call-update) | async-done | bytes 400
  2004.0 64.8 %reduce-scatter.46.cloned.1.call-done = f32[32,14]{1,0:T(8,128)} async-done(((f32[512,14]{1,0:T(8,128)}), f32[32,14]{1,0:T(8,128)}) %reduce-scatter.46.cloned.1.call-update) | async-done | bytes 1808
  2077.3 66.8 %reduce-scatter.36.cloned.1.call-done = f32[100,32]{0,1:T(8,128)} async-done(((f32[100,512]{0,1:T(8,128)}), f32[100,32]{0,1:T(8,128)}) %reduce-scatter.36.cloned.1.call-update) | async-done | bytes 12816 | tf_op jit(solution)/shard_map/reduce_scatter | solution.py:452
  (667 shorter events, 867.8 us)
Async XLA Ops:
  7.2 1780.7 %reduce-scatter.38.cloned.1.call-start = ((), (), s32[]{:S(2)}) async-start(), calls=%async_computation.7 | async-start | bytes 278528
  88.7 24.9 %collective-permute-start.1 = (bf16[1024,512]{0,1:T(8,128)(2,1)}, bf16[1024,512]{0,1:T(8,128)(2,1)S(1)}, u32[]{:S(2)}, u32[]{:S(2)}) collective-permute-start(bf16[1024,512]{0,1:T(8,128)(2,1)} %get-tuple-element.1925), channel_id=1, source_target_pairs={{0,16},{1,17},{2,18},{3,19},{4,20},{5,21},{6,22},{7,23},{8,24},{9,... | collective-permute-start | bytes 3145736 | tf_op jit(solution)/shard_map/while/body/eval_jaxpr/ppermute | solution.py:15
  188.3 24.3 %collective-permute-start.1 = (bf16[1024,512]{0,1:T(8,128)(2,1)}, bf16[1024,512]{0,1:T(8,128)(2,1)S(1)}, u32[]{:S(2)}, u32[]{:S(2)}) collective-permute-start(bf16[1024,512]{0,1:T(8,128)(2,1)} %get-tuple-element.1925), channel_id=1, source_target_pairs={{0,16},{1,17},{2,18},{3,19},{4,20},{5,21},{6,22},{7,23},{8,24},{9,... | collective-permute-start | bytes 3145736 | tf_op jit(solution)/shard_map/while/body/eval_jaxpr/ppermute | solution.py:15
  250.6 78.7 %collective-permute-start = (bf16[1024,512]{1,0:T(8,128)(2,1)}, bf16[1024,512]{1,0:T(8,128)(2,1)}, u32[]{:S(2)}, u32[]{:S(2)}) collective-permute-start(bf16[1024,512]{1,0:T(8,128)(2,1)} %get-tuple-element.1971), channel_id=1, source_target_pairs={{16,0},{17,1},{18,2},{19,3},{20,4},{21,5},{22,6},{23,7},{24,8},{25... | collective-permute-start | bytes 3145736 | tf_op jit(solution)/shard_map/while/body/eval_jaxpr/ppermute | solution.py:15
  347.2 85.4 %collective-permute-start = (bf16[1024,512]{1,0:T(8,128)(2,1)}, bf16[1024,512]{1,0:T(8,128)(2,1)}, u32[]{:S(2)}, u32[]{:S(2)}) collective-permute-start(bf16[1024,512]{1,0:T(8,128)(2,1)} %get-tuple-element.1971), channel_id=1, source_target_pairs={{16,0},{17,1},{18,2},{19,3},{20,4},{21,5},{22,6},{23,7},{24,8},{25... | collective-permute-start | bytes 3145736 | tf_op jit(solution)/shard_map/while/body/eval_jaxpr/ppermute | solution.py:15
  379.8 54.2 %copy-start.24 = (bf16[2,1024,512]{1,2,0:T(8,128)(2,1)S(1)}, bf16[2,1024,512]{1,2,0:T(8,128)(2,1)}, u32[]{:S(2)}) copy-start(bf16[2,1024,512]{1,2,0:T(8,128)(2,1)} %get-tuple-element.2217) | copy-start | bytes 6291460 | tf_op jit(solution)/shard_map/while
  920.3 923.8 %reduce-scatter.40.cloned.1.call-start = ((), (), s32[]{:S(2)}) async-start(), calls=%async_computation.8 | async-start | bytes 278528
  940.4 826.5 %copy-start.110 = (f32[2,512]{1,0:T(2,128)S(1)}, f32[2,512]{1,0:T(2,128)}, u32[]{:S(2)}) copy-start(f32[2,512]{1,0:T(2,128)} %get-tuple-element.805) | copy-start | bytes 12292
  940.5 831.5 %copy-start.97 = (f32[3,512]{1,0:T(4,128)S(1)}, f32[3,512]{1,0:T(4,128)}, u32[]{:S(2)}) copy-start(f32[3,512]{1,0:T(4,128)} %get-tuple-element.810) | copy-start | bytes 18436
  940.5 834.5 %copy-start.94 = (f32[3,512]{1,0:T(4,128)S(1)}, f32[3,512]{1,0:T(4,128)}, u32[]{:S(2)}) copy-start(f32[3,512]{1,0:T(4,128)} %get-tuple-element.811) | copy-start | bytes 18436
  1767.0 231.5 %collective-permute-start.8 = (bf16[32,512]{1,0:T(8,128)(2,1)}, bf16[32,512]{1,0:T(8,128)(2,1)}, u32[]{:S(2)}, u32[]{:S(2)}) collective-permute-start(bf16[32,512]{1,0:T(8,128)(2,1)} %fusion.195), channel_id=1, source_target_pairs={{0,16},{16,0},{1,17},{17,1},{2,18},{18,2},{3,19},{19,3},{4,20},{20... | collective-permute-start | bytes 98312 | tf_op jit(solution)/shard_map/ppermute | solution.py:21
  1767.9 151.7 %reduce-scatter.42.cloned.1.call-start = ((), (), s32[]{:S(2)}) async-start(), calls=%async_computation.9 | async-start | bytes 278528
  1769.9 232.0 %collective-permute-start.6 = (bf16[32,512]{1,0:T(8,128)(2,1)}, bf16[32,512]{1,0:T(8,128)(2,1)}, u32[]{:S(2)}, u32[]{:S(2)}) collective-permute-start(bf16[32,512]{1,0:T(8,128)(2,1)} %fusion.194), channel_id=1, source_target_pairs={{0,16},{16,0},{1,17},{17,1},{2,18},{18,2},{3,19},{19,3},{4,20},{20... | collective-permute-start | bytes 98312 | tf_op jit(solution)/shard_map/ppermute | solution.py:21
  1772.9 221.5 %reduce-scatter.44.cloned.1.call-start = ((), (), s32[]{:S(2)}) async-start(), calls=%async_computation.10 | async-start | bytes 278528
  1775.0 220.8 %collective-permute-start.3 = (bf16[32,512]{1,0:T(8,128)(2,1)}, bf16[32,512]{1,0:T(8,128)(2,1)}, u32[]{:S(2)}, u32[]{:S(2)}) collective-permute-start(bf16[32,512]{1,0:T(8,128)(2,1)} %fusion.193), channel_id=1, source_target_pairs={{0,16},{16,0},{1,17},{17,1},{2,18},{18,2},{3,19},{19,3},{4,20},{20... | collective-permute-start | bytes 98312 | tf_op jit(solution)/shard_map/ppermute | solution.py:21
  1775.8 293.0 %reduce-scatter.46.cloned.1.call-start = ((), (), s32[]{:S(2)}) async-start(), calls=%async_computation.11 | async-start | bytes 278528
  1778.0 292.2 %collective-permute-start.7 = (bf16[32,1024]{1,0:T(8,128)(2,1)}, bf16[32,1024]{1,0:T(8,128)(2,1)}, u32[]{:S(2)}, u32[]{:S(2)}) collective-permute-start(bf16[32,1024]{1,0:T(8,128)(2,1)} %fusion.190), channel_id=1, source_target_pairs={{0,16},{16,0},{1,17},{17,1},{2,18},{18,2},{3,19},{19,3},{4,20},{20... | collective-permute-start | bytes 196616 | tf_op jit(solution)/shard_map/ppermute | solution.py:21
  1780.9 363.1 %reduce-scatter.36.cloned.1.call-start = ((), (), s32[]{:S(2)}) async-start(), calls=%async_computation.6 | async-start | bytes 278528 | tf_op jit(solution)/shard_map/reduce_scatter | solution.py:452
  1783.2 289.2 %collective-permute-start.2 = (bf16[32,1536]{1,0:T(8,128)(2,1)}, bf16[32,1536]{1,0:T(8,128)(2,1)}, u32[]{:S(2)}, u32[]{:S(2)}) collective-permute-start(bf16[32,1536]{1,0:T(8,128)(2,1)} %fusion.187), channel_id=1, source_target_pairs={{0,16},{16,0},{1,17},{17,1},{2,18},{18,2},{3,19},{19,3},{4,20},{20... | collective-permute-start | bytes 294920 | tf_op jit(solution)/shard_map/ppermute | solution.py:21
  1784.1 380.5 %all-reduce.14.cloned.1.call-start = ((), (), s32[]{:S(2)}) async-start(), calls=%async_computation.12 | async-start | bytes 292864 | tf_op jit(solution)/shard_map/psum | solution.py:463
  1995.8 149.7 %collective-permute-start.5 = (bf16[200,512]{1,0:T(8,128)(2,1)}, bf16[200,512]{1,0:T(8,128)(2,1)S(1)}, u32[]{:S(2)}, u32[]{:S(2)}) collective-permute-start(bf16[200,512]{1,0:T(8,128)(2,1)} %fusion.183), channel_id=1, source_target_pairs={{0,16},{16,0},{1,17},{17,1},{2,18},{18,2},{3,19},{19,3},{4,20},{20... | collective-permute-start | bytes 614408 | tf_op jit(solution)/shard_map/ppermute | solution.py:21
  1998.4 76.4 %collective-permute-start.4 = (bf16[32,3200]{1,0:T(8,128)(2,1)}, bf16[32,3200]{1,0:T(8,128)(2,1)S(1)}, u32[]{:S(2)}, u32[]{:S(2)}) collective-permute-start(bf16[32,3200]{1,0:T(8,128)(2,1)} %fusion.182), channel_id=1, source_target_pairs={{0,16},{16,0},{1,17},{17,1},{2,18},{18,2},{3,19},{19,3},{4,20},{20... | collective-permute-start | bytes 614408 | tf_op jit(solution)/shard_map/ppermute | solution.py:21
  2004.0 144.0 %copy-start.72 = (bf16[2,1024,512]{2,1,0:T(8,128)(2,1)S(1)}, bf16[2,1024,512]{2,1,0:T(8,128)(2,1)}, u32[]{:S(2)}) copy-start(bf16[2,1024,512]{2,1,0:T(8,128)(2,1)} %get-tuple-element.791) | copy-start | bytes 6291460
  2145.4 44.5 %all-reduce.16.cloned.1.call-start = ((), (), s32[]{:S(2)}) async-start(), calls=%async_computation.13 | async-start | bytes 2162688 | tf_op jit(solution)/shard_map/psum | solution.py:462
  (142 other events, 888.4 us)
Sparse Core Ops, SparseCore 0:
  920.4 127.3 reduce-scatter.37
  1768.0 76.0 reduce-scatter.39
  1846.9 72.5 reduce-scatter.41
  1921.7 72.6 reduce-scatter.43
  1996.5 72.2 reduce-scatter.45
  2071.6 72.4 reduce-scatter.35
  2148.9 15.6 all-reduce.13
  2168.6 21.2 all-reduce.15
where the time goes:
time: 2230 us; the launch traced here: 2210 us
  blocking collectives  824 us (37%)
  waiting for transfers between devices  501 us (22%)
  matrix products  400 us (18%)
  other arithmetic  247 us (11%)
  local copies, waits for them, and re-layouts  171 us (8%)
  loops' own time  37.1 us (2%)
    unnamed x1, blocking collectives  824 us
    unnamed x13, waiting for transfers between devices  267 us
    ppermute x4, waiting for transfers between devices, from_behind(): return lax.ppermute(array, axis, pairs)  142 us
    dot_general x14, matrix products, product(): return jnp.dot(left_side, right_side, preferred_element_type=jnp.float32)  96.6 us
    reduce_scatter x1, waiting for transfers between devices, per_device(): lax.psum_scatter(decoder_totals[0], ('section', 'dp'), scatter_dimension=...  66.8 us
    add x18, other arithmetic, decoder_turn(): old + new  51.4 us
    dot_general x8, matrix products, one_block(): jnp.einsum('hqk,khd->qhd', weights, value_heads, preferred_element_type=j...  51.3 us
    dot_general x8, matrix products, product_right(): lax.dot_general(left_side, right_side, (((1,), (1,)), ((), ())), preferre...  49.9 us
  transfers between devices with their start and end apart: 19, of which 11 were waited for; matrix products, arithmetic and copies ran while one was open for 6% of the time, Pallas kernels for 0%

commit v1 on v0

v1 whole, which is shorter than its diff:
```python
import functools

import jax
import jax.numpy as jnp
from jax import lax
from jax.experimental import pallas as pl
from jax.experimental.pallas import tpu as pltpu
from jax.sharding import PartitionSpec as P

HEADS = 8
EPSILON = 1e-05
LANES = 128
PAD_ROWS = 128
F32 = jnp.float32
BF16 = jnp.bfloat16
NN = (((1,), (0,)), ((), ()))
NT = (((1,), (1,)), ((), ()))
TN = (((0,), (0,)), ((), ()))
VMEM_BYTES = 56 * 1024 * 1024
ROOT_2_PI = 0.7978845608028654
CUBE = 0.044715


def dot(left, right, dims):
    return lax.dot_general(left, right, dims, preferred_element_type=F32)


def call(kernel, flops, moved, **options):
    return pl.pallas_call(
        kernel,
        compiler_params=pltpu.CompilerParams(vmem_limit_bytes=VMEM_BYTES),
        cost_estimate=pl.CostEstimate(flops=flops, bytes_accessed=moved, transcendentals=0),
        **options,
    )


def shape_of(dims, dtype):
    return jax.ShapeDtypeStruct(dims, dtype)


def whole(array):
    rank = len(array.shape)
    return pl.BlockSpec(array.shape, lambda *_: (0,) * rank, pipeline_mode=pl.Buffered(1))


def normed(residual):
    centre = jnp.mean(residual, axis=-1, keepdims=True)
    centred = residual - centre
    spread = jnp.mean(centred * centred, axis=-1, keepdims=True)
    scale = lax.rsqrt(spread + EPSILON)
    return centred * scale, scale


def normed_back(grad, gain, rows, scale):
    weighted = grad * gain
    return scale * (
        weighted
        - jnp.mean(weighted, axis=-1, keepdims=True)
        - rows * jnp.mean(weighted * rows, axis=-1, keepdims=True)
    )


def gelu_and_slope(value):
    square = value * value
    bend = jnp.tanh(value * (ROOT_2_PI + (ROOT_2_PI * CUBE) * square))
    half = 0.5 + 0.5 * bend
    slope = half + value * (0.5 - 0.5 * bend * bend) * (
        ROOT_2_PI + (3.0 * ROOT_2_PI * CUBE) * square
    )
    return value * half, slope


def column_sum(value):
    return jnp.sum(value, axis=0, keepdims=True)


def attend_kernel(q_ref, k_ref, v_ref, mixed_ref, log_ref):
    count = q_ref.shape[0]
    lane = lax.broadcasted_iota(jnp.int32, (1, LANES), 1)
    keys = k_ref[...]
    values = v_ref[...].T
    queries = q_ref[...] * jnp.asarray(0.125, BF16)
    for head in range(2):
        own = (lane < 64) if head == 0 else (lane >= 64)
        head_keys = jnp.where(own, keys, jnp.zeros_like(keys))
        extended = jnp.concatenate(
            [values[64 * head : 64 * head + 64], jnp.ones((16, count), BF16)], axis=0
        )
        scores = dot(head_keys, queries, NT)
        largest = jnp.max(scores, axis=0, keepdims=True)
        raised = jnp.exp(scores - largest).astype(BF16)
        mixed = dot(extended, raised, NN)
        total = mixed[64:65]
        mixed_ref[pl.ds(64 * head, 64), :] = (mixed[:64] * (1.0 / total)).astype(BF16)
        log_ref[0, pl.ds(head, 1), :] = largest + jnp.log(total)


def attend(packed):
    rows, width = packed.shape[0], packed.shape[1] // 3
    pairs = width // LANES
    column = lambda first: pl.BlockSpec((rows, LANES), lambda j: (0, first + j))
    return call(
        attend_kernel,
        4 * rows * rows * width * 4,
        rows * width * 8,
        grid=(pairs,),
        in_specs=[column(0), column(pairs), column(2 * pairs)],
        out_specs=[
            pl.BlockSpec((LANES, rows), lambda j: (j, 0)),
            pl.BlockSpec((1, 2, rows), lambda j: (j, 0, 0)),
        ],
        out_shape=[shape_of((width, rows), BF16), shape_of((pairs, 2, rows), F32)],
    )(packed, packed, packed)


def attend_back_kernel(block, q_ref, k_ref, v_ref, do_ref, mixed_ref, log_ref, dq_ref, dk_ref, dv_ref):
    count = q_ref.shape[0]
    lane = lax.broadcasted_iota(jnp.int32, (1, LANES), 1)
    keys = k_ref[...]
    values = v_ref[...]
    queries = q_ref[...] * jnp.asarray(0.125, BF16)
    scaled_keys = keys * jnp.asarray(0.125, BF16)
    grads = do_ref[...]
    queries_t = queries.T
    grads_t = grads.T
    logs = log_ref[0].T
    shared = mixed_ref[...].astype(F32) * grads_t.astype(F32)
    inner = jnp.concatenate([column_sum(shared[:64]), column_sum(shared[64:])], axis=0).T
    dq_parts = [[], []]
    dk_parts = []
    dv_parts = []
    for head in range(2):
        own = (lane < 64) if head == 0 else (lane >= 64)
        head_queries = jnp.where(own, queries, jnp.zeros_like(queries))
        head_grads = jnp.where(own, grads, jnp.zeros_like(grads))
        dk = None
        dv = None
        for start in range(0, count, block):
            part = slice(start, start + block)
            scores = dot(head_queries[part], keys, NT)
            probs = jnp.exp(scores - logs[part, head : head + 1])
            grad_probs = dot(head_grads[part], values, NT)
            grad_scores = (probs * (grad_probs - inner[part, head : head + 1])).astype(BF16)
            new_v = dot(grads_t[64 * head : 64 * head + 64, part], probs.astype(BF16), NN)
            new_k = dot(queries_t[64 * head : 64 * head + 64, part], grad_scores, NN)
            dv = new_v if dv is None else dv + new_v
            dk = new_k if dk is None else dk + new_k
            dq_parts[head].append(dot(grad_scores, scaled_keys, NN))
        dk_parts.append(dk)
        dv_parts.append(dv)
    dk_ref[...] = jnp.concatenate(dk_parts, axis=0).T.astype(BF16)
    dv_ref[...] = jnp.concatenate(dv_parts, axis=0).T.astype(BF16)
    for index in range(count // block):
        dq_ref[pl.ds(index * block, block), :] = jnp.where(
            lane < 64, dq_parts[0][index], dq_parts[1][index]
        ).astype(BF16)


def attend_back(packed, grad_mixed, mixed, logs):
    rows, width = packed.shape[0], packed.shape[1] // 3
    pairs = width // LANES
    column = lambda first: pl.BlockSpec((rows, LANES), lambda j: (0, first + j))
    return call(
        functools.partial(attend_back_kernel, 256),
        10 * rows * rows * width * 3,
        rows * width * 16,
        grid=(pairs,),
        in_specs=[
            column(0),
            column(pairs),
            column(2 * pairs),
            column(0),
            pl.BlockSpec((LANES, rows), lambda j: (j, 0)),
            pl.BlockSpec((1, 2, rows), lambda j: (j, 0, 0)),
        ],
        out_specs=[column(0)] * 3,
        out_shape=[shape_of((rows, width), BF16)] * 3,
    )(packed, packed, packed, grad_mixed, mixed, logs)


def encode_rows_kernel(
    x_ref, mixed_ref, combine_ref, expand_ref, reduce_ref, gain_ref, shift_ref, memory_w_ref,
    first_ref, low_ref, active_ref, slope_ref, second_ref, memory_ref, pair_ref,
):
    residual = x_ref[...].astype(F32) + dot(mixed_ref[...], combine_ref[...], TN)
    first_ref[...] = residual
    rows, _ = normed(residual)
    first = rows * gain_ref[0:1, :] + shift_ref[0:1, :]
    low = first.astype(BF16)
    low_ref[...] = low
    total = first
    hidden_size = expand_ref.shape[1]
    step = hidden_size // 5
    for start in range(0, hidden_size, step):
        part = pl.ds(start, step)
        active, slope = gelu_and_slope(dot(low, expand_ref[:, part], NN))
        active = active.astype(BF16)
        active_ref[:, part] = active
        slope_ref[:, part] = slope.astype(BF16)
        total = total + dot(active, reduce_ref[part, :], NN)
    second_ref[...] = total
    rows, _ = normed(total)
    memory = (rows * gain_ref[1:2, :] + shift_ref[1:2, :]).astype(BF16)
    memory_ref[...] = memory
    pair_ref[...] = dot(memory, memory_w_ref[...], NN).astype(BF16)


def encode_rows(x, mixed, combine_w, expand_w, reduce_w, gains, shifts, memory_w):
    rows, width = x.shape
    hidden = expand_w.shape[1]
    block = 256
    line = lambda size: pl.BlockSpec((block, size), lambda i: (i, 0))
    sizes = [(width, F32), (width, BF16), (hidden, BF16), (hidden, BF16), (width, F32), (width, BF16), (2 * width, BF16)]
    return call(
        encode_rows_kernel,
        2 * rows * width * (2 * hidden + 3 * width),
        rows * (hidden * 4 + width * 18) + 8 * width * hidden,
        grid=(rows // block,),
        in_specs=[line(width), pl.BlockSpec((width, block), lambda i: (0, i))]
        + [whole(item) for item in (combine_w, expand_w, reduce_w, gains, shifts, memory_w)],
        out_specs=[line(size) for size, _ in sizes],
        out_shape=[shape_of((rows, size), kind) for size, kind in sizes],
    )(x, mixed, combine_w, expand_w, reduce_w, gains, shifts, memory_w)


def encode_back_kernel(
    pair_ref, first_ref, second_ref, slope_ref, combine_ref, expand_ref, reduce_ref, gain_ref, memory_w_ref,
    grad_memory_ref, branch_ref, hidden_ref, resid_ref, low_ref, mixed_ref, sums_ref,
):
    grad_memory = dot(pair_ref[...], memory_w_ref[...], NT).astype(BF16)
    grad_memory_ref[...] = grad_memory
    grad_last = grad_memory.astype(F32)
    rows, scale = normed(second_ref[...])
    gain_last = column_sum(grad_last * rows)
    shift_last = column_sum(grad_last)
    grad_second = normed_back(grad_last, gain_ref[1:2, :], rows, scale)
    branch = grad_second.astype(BF16)
    branch_ref[...] = branch
    total = grad_second
    hidden_size = expand_ref.shape[1]
    step = hidden_size // 5
    for start in range(0, hidden_size, step):
        part = pl.ds(start, step)
        grad_active = dot(branch, reduce_ref[part, :], NT)
        grad_hidden = (grad_active * slope_ref[:, part].astype(F32)).astype(BF16)
        hidden_ref[:, part] = grad_hidden
        total = total + dot(grad_hidden, expand_ref[:, part], NT)
    rows, scale = normed(first_ref[...])
    gain_first = column_sum(total * rows)
    shift_first = column_sum(total)
    grad_first = normed_back(total, gain_ref[0:1, :], rows, scale)
    resid_ref[...] = grad_first
    low = grad_first.astype(BF16)
    low_ref[...] = low
    mixed_ref[...] = dot(low, combine_ref[...], NT).astype(BF16)
    fresh = jnp.concatenate(
        [gain_first, gain_last, shift_first, shift_last, jnp.zeros((4, gain_first.shape[1]), F32)], axis=0
    )

    @pl.when(pl.program_id(0) == 0)
    def _():
        sums_ref[...] = fresh

    @pl.when(pl.program_id(0) > 0)
    def _():
        sums_ref[...] += fresh


def encode_back(grad_pair, first, second, slope, combine_w, expand_w, reduce_w, gains, memory_w):
    rows, width = first.shape
    hidden = expand_w.shape[1]
    block = 256
    line = lambda size: pl.BlockSpec((block, size), lambda i: (i, 0))
    sizes = [(width, BF16), (width, BF16), (hidden, BF16), (width, F32), (width, BF16), (width, BF16)]
    return call(
        encode_back_kernel,
        2 * rows * width * (2 * hidden + 3 * width),
        rows * (hidden * 4 + width * 18) + 8 * width * hidden,
        grid=(rows // block,),
        in_specs=[line(2 * width), line(width), line(width), line(hidden)]
        + [whole(item) for item in (combine_w, expand_w, reduce_w, gains, memory_w)],
        out_specs=[line(size) for size, _ in sizes] + [pl.BlockSpec((8, width), lambda i: (0, 0))],
        out_shape=[shape_of((rows, size), kind) for size, kind in sizes] + [shape_of((8, width), F32)],
    )(grad_pair, first, second, slope, combine_w, expand_w, reduce_w, gains, memory_w)


def by_rows_kernel(half, left_ref, right_ref, out_ref):
    result = dot(left_ref[...], right_ref[...], TN).astype(BF16)
    for start in range(0, result.shape[0], 2 * half):
        for core in range(2):
            out_ref[core, pl.ds(start // 2, half), :] = result[
                start + core * half : start + core * half + half
            ]


def gradient_by_rows(left, right, step):
    count, rows = left.shape
    columns = right.shape[1]
    return call(
        functools.partial(by_rows_kernel, 16),
        2 * count * rows * columns,
        2 * (count * (rows + columns) + rows * columns),
        grid=(columns // step,),
        in_specs=[whole(left), pl.BlockSpec((count, step), lambda i: (0, i))],
        out_specs=pl.BlockSpec((2, rows // 2, step), lambda i: (0, 0, i)),
        out_shape=shape_of((2, rows // 2, columns), BF16),
    )(left, right)


def by_columns_kernel(left_ref, right_ref, out_ref):
    result = dot(left_ref[...], right_ref[...], TN).astype(BF16)
    half = result.shape[1] // 2
    out_ref[0] = result[:, :half]
    out_ref[1] = result[:, half:]


def gradient_by_columns(left, right, step):
    count, rows = left.shape
    columns = right.shape[1]
    return call(
        by_columns_kernel,
        2 * count * rows * columns,
        2 * (count * (rows + columns) + rows * columns),
        grid=(rows // step,),
        in_specs=[pl.BlockSpec((count, step), lambda i: (0, i)), whole(right)],
        out_specs=pl.BlockSpec((2, step, columns // 2), lambda i: (0, i, 0)),
        out_shape=shape_of((2, rows, columns // 2), BF16),
    )(left, right)


def stacked(rows):
    lane = lax.broadcasted_iota(jnp.int32, (1, rows.shape[1]), 1)
    return jnp.concatenate(
        [jnp.where((lane >= 64 * h) & (lane < 64 * h + 64), rows, jnp.zeros_like(rows)) for h in range(4)],
        axis=0,
    )


def unstacked(rows):
    lane = lax.broadcasted_iota(jnp.int32, (1, rows.shape[1]), 1)
    count = rows.shape[0] // 4
    result = rows[:count]
    for h in range(1, 4):
        result = jnp.where(lane >= 64 * h, rows[h * count : h * count + count], result)
    return result


def few_attend(queries, keys, values, valid):
    mixed = []
    kept = []
    for half in range(2):
        part = slice(256 * half, 256 * half + 256)
        scores = dot(stacked(queries[:, part] * jnp.asarray(0.125, BF16)), keys[:, part], NT)
        if valid < scores.shape[1]:
            column = lax.broadcasted_iota(jnp.int32, (1, scores.shape[1]), 1)
            scores = jnp.where(column < valid, scores, -1e30)
        raised = jnp.exp(scores - jnp.max(scores, axis=1, keepdims=True))
        probs = raised * (1.0 / jnp.sum(raised, axis=1, keepdims=True))
        mixed.append(unstacked(dot(probs.astype(BF16), values[:, part], NN)))
        kept.append(probs)
    return jnp.concatenate(mixed, axis=1).astype(BF16), kept


def few_attend_back(queries, keys, values, kept, grads):
    dq, dk, dv = [], [], []
    for half in range(2):
        part = slice(256 * half, 256 * half + 256)
        probs = kept[half]
        own_queries = stacked(queries[:, part] * jnp.asarray(0.125, BF16))
        own_grads = stacked(grads[:, part])
        grad_probs = dot(own_grads, values[:, part], NT)
        product = probs * grad_probs
        grad_scores = (product - probs * jnp.sum(product, axis=1, keepdims=True)).astype(BF16)
        dv.append(dot(probs.astype(BF16), own_grads, TN))
        dk.append(dot(grad_scores, own_queries, TN))
        dq.append(unstacked(dot(grad_scores, keys[:, part], NN)) * 0.125)
    return jnp.concatenate(dq, axis=1), jnp.concatenate(dk, axis=1), jnp.concatenate(dv, axis=1)


def self_block(starts, project_w, combine_w, gain, shift, valid):
    width = starts.shape[1]
    packed = dot(starts, project_w, NN).astype(BF16)
    queries, keys, values = (packed[:, i * width : (i + 1) * width] for i in range(3))
    mixed, kept = few_attend(queries, keys, values, valid)
    residual = starts.astype(F32) + dot(mixed, combine_w, NN)
    rows, scale = normed(residual)
    return queries, keys, values, mixed, kept, rows, scale, rows * gain + shift


def decode_kernel(
    valid, joints,
    starts_ref, project_ref, combine_ref, query_ref, cross_ref, expand_ref, reduce_ref, gain_ref, shift_ref,
    head_ref, pair_ref, target_ref, arm_ref,
    grad_pair_ref, second_low_ref, hidden_ref, active_ref, branch_ref, cross_grad_ref, small_ref, query_grad_ref,
    head_grad_ref, sums_ref,
):
    width = starts_ref.shape[1]
    first = self_block(
        starts_ref[...], project_ref[...], combine_ref[...], gain_ref[0:1, :], shift_ref[0:1, :], valid
    )[-1]
    queries = dot(first.astype(BF16), query_ref[...], NN).astype(BF16)
    keys = pair_ref[:, :width]
    values = pair_ref[:, width:]
    mixed, kept = few_attend(queries, keys, values, keys.shape[0])
    second_rows, second_scale = normed(first + dot(mixed, cross_ref[...], NN))
    second = second_rows * gain_ref[1:2, :] + shift_ref[1:2, :]
    second_low = second.astype(BF16)
    second_low_ref[...] = second_low
    hidden_size = expand_ref.shape[1]
    step = hidden_size // 5
    total = second
    slopes = []
    for start in range(0, hidden_size, step):
        part = pl.ds(start, step)
        active, slope = gelu_and_slope(dot(second_low, expand_ref[:, part], NN))
        slopes.append(slope)
        active = active.astype(BF16)
        active_ref[:, part] = active
        total = total + dot(active, reduce_ref[part, :], NN)
    third_rows, third_scale = normed(total)
    third_low = (third_rows * gain_ref[2:3, :] + shift_ref[2:3, :]).astype(BF16)
    misfit = dot(third_low, head_ref[...], NN) - target_ref[...]
    arms = arm_ref[0]
    row = lax.broadcasted_iota(jnp.int32, misfit.shape, 0)
    joint = lax.broadcasted_iota(jnp.int32, misfit.shape, 1)
    factor = 2.0 / jnp.full((1, 1), arms, jnp.int32).astype(F32)
    used = (row < valid) & (joint < joints // 2 * arms)
    grad_pred = jnp.where(used, factor * misfit * lax.rsqrt(misfit * misfit + 1.0), 0.0).astype(BF16)
    head_grad_ref[...] = dot(third_low, grad_pred, TN)
    grad_third = dot(grad_pred, head_ref[...], NT)
    gain_third = column_sum(grad_third * third_rows)
    shift_third = column_sum(grad_third)
    total = normed_back(grad_third, gain_ref[2:3, :], third_rows, third_scale)
    branch = total.astype(BF16)
    branch_ref[...] = branch
    for index, start in enumerate(range(0, hidden_size, step)):
        part = pl.ds(start, step)
        grad_hidden = (dot(branch, reduce_ref[part, :], NT) * slopes[index]).astype(BF16)
        hidden_ref[:, part] = grad_hidden
        total = total + dot(grad_hidden, expand_ref[:, part], NT)
    gain_second = column_sum(total * second_rows)
    shift_second = column_sum(total)
    grad_second = normed_back(total, gain_ref[1:2, :], second_rows, second_scale)
    small_ref[...] = grad_second
    branch = grad_second.astype(BF16)
    cross_grad_ref[...] = dot(mixed, branch, TN).astype(BF16)
    grad_mixed = dot(branch, cross_ref[...], NT).astype(BF16)
    dq, dk, dv = few_attend_back(queries, keys, values, kept, grad_mixed)
    query_grad_ref[...] = dq.astype(BF16).astype(F32)
    grad_pair_ref[:, :width] = dk.astype(BF16)
    grad_pair_ref[:, width:] = dv.astype(BF16)
    sums_ref[...] = jnp.concatenate(
        [gain_second, gain_third, shift_second, shift_third, jnp.zeros((4, width), F32)], axis=0
    )


def decode(valid, joints, starts, weights, pair, target, arm):
    project_w, combine_w, query_w, cross_w, expand_w, reduce_w, gains, shifts, head_w = weights
    count, width = starts.shape
    hidden = expand_w.shape[1]
    shapes = [
        (pair.shape, BF16),
        ((count, width), BF16),
        ((count, hidden), BF16),
        ((count, hidden), BF16),
        ((count, width), BF16),
        ((width, width), BF16),
        ((count, width), F32),
        ((count, width), F32),
        (head_w.shape, F32),
        ((8, width), F32),
    ]
    arrays = (starts, project_w, combine_w, query_w, cross_w, expand_w, reduce_w, gains, shifts, head_w, pair, target)
    return call(
        functools.partial(decode_kernel, valid, joints),
        8 * count * width * hidden * 4,
        16 * 1024 * 1024,
        in_specs=[pl.BlockSpec(memory_space=pltpu.VMEM)] * len(arrays) + [pl.BlockSpec(memory_space=pltpu.SMEM)],
        out_specs=[pl.BlockSpec(memory_space=pltpu.VMEM)] * len(shapes),
        out_shape=[shape_of(dims, kind) for dims, kind in shapes],
    )(*arrays, arm)


def decode_start_back_kernel(
    valid,
    starts_ref, project_ref, combine_ref, query_ref, gain_ref, shift_ref, resid_ref, query_grad_ref,
    start_grad_ref, project_grad_ref, combine_grad_ref, query_w_grad_ref, sums_ref,
):
    starts = starts_ref[...]
    project_w = project_ref[...]
    queries, keys, values, mixed, kept, rows, scale, first = self_block(
        starts, project_w, combine_ref[...], gain_ref[0:1, :], shift_ref[0:1, :], valid
    )
    low = query_grad_ref[...].astype(BF16)
    query_w_grad_ref[...] = dot(first.astype(BF16), low, TN)
    grad_first = resid_ref[...] + dot(low, query_ref[...], NT)
    gain_sum = column_sum(grad_first * rows)
    shift_sum = column_sum(grad_first)
    grad_resid = normed_back(grad_first, gain_ref[0:1, :], rows, scale)
    branch = grad_resid.astype(BF16)
    combine_grad_ref[...] = dot(mixed, branch, TN)
    grad_mixed = dot(branch, combine_ref[...], NT).astype(BF16)
    dq, dk, dv = few_attend_back(queries, keys, values, kept, grad_mixed)
    grad_packed = jnp.concatenate([dq, dk, dv], axis=1).astype(BF16)
    project_grad_ref[...] = dot(starts, grad_packed, TN)
    start_grad_ref[...] = grad_resid + dot(grad_packed, project_w, NT)
    sums_ref[...] = jnp.concatenate([gain_sum, shift_sum, jnp.zeros((6, gain_sum.shape[1]), F32)], axis=0)


def decode_start_back(valid, starts, project_w, combine_w, query_w, gains, shifts, resid, query_grad):
    count, width = starts.shape
    arrays = (starts, project_w, combine_w, query_w, gains, shifts, resid, query_grad)
    shapes = [(count, width), (width, 3 * width), (width, width), (width, width), (8, width)]
    return call(
        functools.partial(decode_start_back_kernel, valid),
        2 * count * width * width * 20,
        8 * 1024 * 1024,
        in_specs=[pl.BlockSpec(memory_space=pltpu.VMEM)] * len(arrays),
        out_specs=[pl.BlockSpec(memory_space=pltpu.VMEM)] * len(shapes),
        out_shape=[shape_of(dims, F32) for dims in shapes],
    )(*arrays)


def episode(x, target, arm, weights):
    (
        encoder_project, encoder_combine, encoder_expand, encoder_reduce, encoder_gains, encoder_shifts,
        starts, decoder_project, decoder_combine, cross_query, cross_memory, cross_combine,
        decoder_expand, decoder_reduce, decoder_gains, decoder_shifts, head,
    ) = weights
    valid, joints = starts.shape[0], head.shape[1]
    packed = dot(x, encoder_project, NN).astype(BF16)
    mixed, logs = attend(packed)
    first, first_low, active, slope, second, memory, pair = encode_rows(
        x, mixed, encoder_combine, encoder_expand, encoder_reduce, encoder_gains, encoder_shifts, cross_memory
    )
    padded = jnp.pad(starts, ((0, PAD_ROWS - valid), (0, 0)))
    wide_head = jnp.pad(head, ((0, 0), (0, LANES - joints)))
    wide_target = jnp.pad(target, ((0, PAD_ROWS - valid), (0, LANES - joints)))
    (
        grad_pair, second_low, grad_hidden_d, active_d, branch_d, cross_grad, resid_d, query_grad, head_grad, sums_d,
    ) = decode(
        valid, joints, padded,
        (
            decoder_project, decoder_combine, cross_query, cross_combine, decoder_expand, decoder_reduce,
            decoder_gains, decoder_shifts, wide_head,
        ),
        pair, wide_target, arm,
    )
    expand_d = gradient_by_rows(second_low, grad_hidden_d, 640)
    reduce_d = gradient_by_columns(active_d, branch_d, 640)
    grad_memory, branch, grad_hidden, resid, low, grad_mixed, sums_e = encode_back(
        grad_pair, first, second, slope, encoder_combine, encoder_expand, encoder_reduce, encoder_gains, cross_memory
    )
    memory_w_grad = gradient_by_rows(memory, grad_pair, 512)
    reduce_e = gradient_by_columns(active, branch, 640)
    expand_e = gradient_by_rows(first_low, grad_hidden, 640)
    combine_e = gradient_by_rows(mixed.T, low, 512)
    dq, dk, dv = attend_back(packed, grad_mixed, mixed, logs)
    grad_packed = jnp.concatenate([dq, dk, dv], axis=1)
    project_e = gradient_by_rows(x, grad_packed, 512)
    grad_x = (resid + dot(grad_packed, encoder_project, NT)).astype(BF16)
    cross_rows = cross_grad.reshape(-1, 2, 16, cross_grad.shape[1]).transpose(1, 0, 2, 3).reshape(2, -1, cross_grad.shape[1])
    return memory, grad_x, grad_memory, {
        "encoder_project": project_e,
        "encoder_combine": combine_e,
        "encoder_expand": expand_e,
        "encoder_reduce": reduce_e,
        "decoder_expand": expand_d,
        "decoder_reduce": reduce_d,
        "cross_memory": memory_w_grad,
        "cross_combine": cross_rows,
        "sums_e": sums_e,
        "sums_d": sums_d,
        "resid_d": resid_d,
        "query_d": query_grad,
        "head": head_grad[:, :joints],
    }


def swap(value, axis, bit):
    pairs = [(i, i ^ (1 << bit)) for i in range(lax.axis_size(axis))]
    return lax.ppermute(value, axis, pairs)


class Shards:
    def __init__(self):
        self.bits = [("section", b) for b in reversed(range(lax.axis_size("section").bit_length() - 1))]
        self.bits += [("dp", b) for b in reversed(range(lax.axis_size("dp").bit_length() - 1))]
        self.mine = [(lax.axis_index(axis) >> bit) & 1 for axis, bit in self.bits]

    def take(self, term, fixed):
        starts, sizes = [], []
        for dim, size in enumerate(term.shape):
            if dim in fixed and size == 2:
                starts.append(fixed[dim])
                sizes.append(1)
            else:
                starts.append(0)
                sizes.append(size)
        return lax.dynamic_slice(term, starts, sizes).astype(F32)

    def total(self, terms, fixed):
        value = self.take(terms[0], fixed)
        for term in terms[1:]:
            value = value + self.take(term, fixed)
        return value

    def reduce(self, halves, order):
        core = lax.axis_index("rep")
        rows = halves.shape[1] >> len(self.bits)
        lead = (2,) * len(self.bits)
        shape = lead + (rows, halves.shape[2])
        pick = lambda index: lax.dynamic_index_in_dim(halves, index, 0, keepdims=False).reshape(shape)
        terms = [pick(core), swap(pick(1 - core), "rep", 0)]
        fixed = {}
        for dim in order:
            axis, bit = self.bits[dim]
            sent = self.total(terms, {**fixed, dim: 1 - self.mine[dim]}).astype(BF16)
            terms.append(swap(sent, axis, bit))
            fixed[dim] = self.mine[dim]
        return self.total(terms, fixed).astype(BF16).reshape(rows, halves.shape[2])


def both_cores(own, axis):
    other = swap(own, "rep", 0)
    first = lax.axis_index("rep") == 0
    return jnp.concatenate(
        [jnp.where(first, own, other), jnp.where(first, other, own)], axis=axis
    ).astype(F32)


def everywhere(value, kind):
    for axis in ("rep", "section", "dp"):
        for bit in range(lax.axis_size(axis).bit_length() - 1):
            low = value.astype(kind)
            value = low.astype(F32) + swap(low, axis, bit).astype(F32)
    return value


def from_halves_rows(halves):
    rows, columns = 2 * halves.shape[1], halves.shape[2]
    return halves.reshape(2, -1, 16, columns).transpose(1, 0, 2, 3).reshape(rows, columns)


def from_halves_columns(halves):
    return jnp.concatenate([halves[0], halves[1]], axis=1)


def plain_scatter(full):
    part = lax.psum_scatter(full.astype(F32), ("section", "dp"), scatter_dimension=0, tiled=True)
    return lax.psum(part, "rep")


ROW_GROUPS = {
    "decoder_expand": (0, 3, 2, 1),
    "cross": (3, 2, 1, 0),
    "encoder_expand": (2, 3, 1, 0),
    "encoder_attend": (3, 2, 0, 1),
}
COLUMN_GROUPS = {"decoder_reduce": (3, 0, 2, 1), "encoder_reduce": (3, 2, 1, 0)}


def per_device(x, targets, arms, *weights):
    section = lax.axis_index("section")
    sections = lax.axis_size("section")
    lanes = lax.axis_size("dp")
    count = x.shape[0] // sections
    starts, head = weights[6], weights[16]
    valid, joints = starts.shape[0], head.shape[1]
    width = starts.shape[1]
    memories, grads_x, grads_m, sums = [], [], [], None
    for index in range(count):
        place = section * count + index
        pick = lambda array: lax.dynamic_index_in_dim(array, place, 0, keepdims=False)
        memory, grad_x, grad_memory, fresh = episode(
            pick(x), pick(targets), lax.dynamic_slice(arms, (place,), (1,)), weights
        )
        memories.append(memory)
        grads_x.append(grad_x)
        grads_m.append(grad_memory)
        sums = fresh if sums is None else {
            name: (sums[name].astype(F32) + fresh[name].astype(F32)).astype(fresh[name].dtype) for name in fresh
        }
    first = section == 0
    memory = jnp.stack(memories)
    other = swap(memory, "section", 0)
    memory_out = jnp.concatenate([jnp.where(first, memory, other), jnp.where(first, other, memory)])
    grad_m = jnp.stack(grads_m)
    grad_x = jnp.stack(grads_x)
    from_first = lax.ppermute(grad_m, "section", [(0, 1)])
    from_second = lax.ppermute(grad_x, "section", [(1, 0)])
    slab = jnp.concatenate([jnp.where(first, grad_x, from_first), jnp.where(first, from_second, grad_m)])[None]

    place = section * lanes + lax.axis_index("dp")
    own = width // (sections * lanes)
    columns_of = lambda array: lax.dynamic_slice_in_dim(array, place * own, own, 1)
    rows_of = lambda array: lax.dynamic_slice_in_dim(array, place * own, own, 0)

    small_low = everywhere(jnp.concatenate([sums["resid_d"][:104], sums["query_d"][:104]]), BF16)
    rest = PAD_ROWS - 104
    resid_d = jnp.pad(small_low[:104], ((0, rest), (0, 0)))
    query_d = jnp.pad(small_low[104:], ((0, rest), (0, 0)))
    small = everywhere(
        jnp.concatenate([sums["sums_d"][:4], sums["sums_e"][:4], sums["head"].T]), F32
    )
    head_sum = small[8:].T
    start_grad, project_d, combine_d, query_w, sums_s = decode_start_back(
        valid, jnp.pad(starts, ((0, PAD_ROWS - valid), (0, 0))), weights[7], weights[8], weights[9],
        weights[14], weights[15], resid_d, query_d,
    )
    gains_d = jnp.concatenate([sums_s[0:1], small[0:2]])
    shifts_d = jnp.concatenate([sums_s[1:2], small[2:4]])

    groups = {
        "decoder_expand": sums["decoder_expand"],
        "cross": jnp.concatenate([sums["cross_memory"], sums["cross_combine"]], axis=2),
        "encoder_expand": sums["encoder_expand"],
        "encoder_attend": jnp.concatenate([sums["encoder_project"], sums["encoder_combine"]], axis=2),
        "decoder_reduce": sums["decoder_reduce"],
        "encoder_reduce": sums["encoder_reduce"],
    }
    done = {}
    if own == 32:
        shards = Shards()
        for name, order in ROW_GROUPS.items():
            done[name] = both_cores(shards.reduce(groups[name], order), 0)
        for name, order in COLUMN_GROUPS.items():
            done[name] = both_cores(shards.reduce(groups[name], order), 1)
    else:
        for name in ROW_GROUPS:
            done[name] = plain_scatter(from_halves_rows(groups[name]))
        for name in COLUMN_GROUPS:
            done[name] = plain_scatter(from_halves_columns(groups[name]))
    return (
        memory_out,
        slab,
        done["encoder_attend"][:, : 3 * width],
        done["encoder_attend"][:, 3 * width :],
        done["encoder_expand"],
        done["encoder_reduce"],
        columns_of(small[4:6]),
        columns_of(small[6:8]),
        columns_of(start_grad[:valid]),
        rows_of(project_d),
        rows_of(combine_d),
        rows_of(query_w),
        done["cross"][:, : 2 * width],
        done["cross"][:, 2 * width :],
        done["decoder_expand"],
        done["decoder_reduce"],
        columns_of(gains_d),
        columns_of(shifts_d),
        rows_of(head_sum),
    )


def solution(mesh):
    spread = ("section", "dp")
    rows = P(spread, None)
    columns = P(None, spread)
    return jax.shard_map(
        per_device,
        mesh=mesh,
        in_specs=(P(("dp", "rep"), None, None), P(("dp", "rep"), None, None), P(("dp", "rep"))) + (P(),) * 17,
        out_specs=(
            P(("dp", "rep"), None, None),
            P("section", ("dp", "rep"), None, None),
            rows, rows, rows, rows, columns, columns, columns,
            rows, rows, rows, rows, rows, rows, rows, columns, columns, rows,
        ),
        check_vma=False,
    )
```

time: 2230 us -> 436 us (0.20)
  blocking collectives: 824 us -> 0 us
  matrix products: 400 us -> 6.61 us
  waiting for transfers between devices: 501 us -> 133 us
  other arithmetic: 247 us -> 45.9 us
  Pallas kernels: 0 us -> 146 us
  local copies, waits for them, and re-layouts: 171 us -> 33.4 us
  starting transfers between devices: 11.7 us -> 61.3 us
  loops' own time: 37.1 us -> 0 us
    unnamed x1 -> x0, blocking collectives: 824 us -> none
    dot_general x62 -> x2, matrix products: 362 us -> 6.61 us  [dot(): return lax.dot_general(left, right, dims, preferred_element_type=F32)]
    unnamed x13 -> x0, waiting for transfers between devices: 267 us -> none
    pallas_call x0 -> x13, Pallas kernels: none -> 146 us  [the longest x5 27.5 us: gradient_by_rows(): call(functools.partial(by_rows_kernel, 16), 2 * count * rows * columns, 2...]
    add x28 -> x6, other arithmetic: 91.3 us -> 1.81 us  [everywhere(): value = low.astype(F32) + swap(low, axis, bit).astype(F32)]
    convert_element_type x38 -> x34, other arithmetic: 98.6 us -> 27.7 us  [the longest x24 23.2 us: reduce(): sent = self.total(terms, {**fixed, dim: 1 - self.mine[dim]}).astype(BF16)]
    reduce_scatter x1 -> x0, waiting for transfers between devices: 66.8 us -> none  [per_device(): lax.psum_scatter(decoder_totals[0], ('section', 'dp'), scatter_dimension=...]
    while x189 -> x0, local copies, waits for them, and re-layouts: 52.6 us -> none
  transfers between devices with their start and end apart: 19 -> 49, of which waited for: 11 -> 23; matrix products, arithmetic and copies ran while one was open for 6% -> 18% of each run, Pallas kernels for 0% -> 26%
where the time goes in v1:
time: 436 us; the launch traced here: 428 us
  Pallas kernels  146 us (33%)
  waiting for transfers between devices  133 us (31%)
  starting transfers between devices  61.3 us (14%)
  other arithmetic  45.9 us (11%)
  local copies, waits for them, and re-layouts  33.4 us (8%)
  matrix products  6.61 us (2%)
    ppermute x47, waiting for transfers between devices, swap(): return lax.ppermute(value, axis, pairs)  133 us
    ppermute x47, starting transfers between devices, swap(): return lax.ppermute(value, axis, pairs)  57 us
    pallas_call x5, Pallas kernels, gradient_by_rows(): call(functools.partial(by_rows_kernel, 16), 2 * count * rows * columns, 2...  27.5 us
    convert_element_type x24, other arithmetic, reduce(): sent = self.total(terms, {**fixed, dim: 1 - self.mine[dim]}).astype(BF16)  23.2 us
    pallas_call x1, Pallas kernels, attend_back(): call(functools.partial(attend_back_kernel, 256), 10 * rows * rows * width...  22.9 us
    pallas_call x1, Pallas kernels, encode_rows(): call(encode_rows_kernel, 2 * rows * width * (2 * hidden + 3 * width), row...  22.3 us
    pallas_call x1, Pallas kernels, encode_back(): call(encode_back_kernel, 2 * rows * width * (2 * hidden + 3 * width), row...  19.5 us
    pallas_call x1, Pallas kernels, decode(): call(functools.partial(decode_kernel, valid, joints), 8 * count * width *...  18 us
  transfers between devices with their start and end apart: 49, of which 23 were waited for; matrix products, arithmetic and copies ran while one was open for 18% of the time, Pallas kernels for 26%

profile of v1, /device:TPU:0, one launch (start us, length us, event | category | flops | bytes accessed | tf_op | source)
XLA Modules:
  0.0 427.6 jit_solution(8743375880745850916)
XLA Ops:
  7.1 14.7 %shard_map.339 = (bf16[512,1024]{1,0:T(8,128)(2,1)}, f32[4,2,1024]{2,1,0:T(2,128)}) custom-call(bf16[1024,1536]{1,0:T(8,128)(2,1)} %convolution_convert_fusion.q_ref.k_ref.v_ref, bf16[1024,1536]{1,0:T(8,128)(2,1)} %convolution_convert_fusion.q_ref.k_ref.v_ref, bf16[1024,1536]{1,0:T(8,128)(2,1)} %convolution_convert_fusion.q_ref.k_ref.v_ref), custom_call_target="tpu_custom_call" | custom-call | flops 8589934592 | bytes 4194304 | tf_op jit(solution)/shard_map/pallas_call | solution.py:102
  21.9 22.3 %shard_map.340 = (f32[1024,512]{1,0:T(8,128)}, bf16[1024,512]{1,0:T(8,128)(2,1)}, bf16[1024,3200]{1,0:T(8,128)(2,1)}, bf16[1024,3200]{1,0:T(8,128)(2,1)}, f32[10...) custom-call(bf16[1024,512]{1,0:T(8,128)(2,1)} %copy-done.10, ...), custom_call_target="tpu_custom_call" | custom-call | flops 8321499136 | bytes 35651584 | tf_op jit(solution)/shard_map/pallas_call | solution.py:214
  50.0 18.0 %shard_map.341 = (bf16[1024,1024]{1,0:T(8,128)(2,1)}, bf16[128,512]{1,0:T(8,128)(2,1)}, bf16[128,3200]{1,0:T(8,128)(2,1)}, bf16[128,3200]{1,0:T(8,128)(2,1)}, bf...) custom-call(bf16[128,512]{1,0:T(8,128)(2,1)} %pad.20.starts_ref, ...), custom_call_target="tpu_custom_call" | custom-call | flops 6710886400 | bytes 16777216 | tf_op jit(solution)/shard_map/pallas_call | solution.py:474
  77.5 19.5 %shard_map.342 = (bf16[1024,512]{1,0:T(8,128)(2,1)}, bf16[1024,512]{1,0:T(8,128)(2,1)}, bf16[1024,3200]{1,0:T(8,128)(2,1)}, f32[1024,512]{1,0:T(8,128)}, bf16[10...) custom-call(bf16[1024,1024]{1,0:T(8,128)(2,1)} %get-tuple-element.56.pair_ref.right_ref, ...), custom_call_target="tpu_custom_call" | custom-call | flops 8321499136 | bytes 35651584 | tf_op jit(solution)/shard_map/pallas_call | solution.py:275
  100.7 22.9 %shard_map.343 = (bf16[1024,512]{1,0:T(8,128)(2,1)}, bf16[1024,512]{1,0:T(8,128)(2,1)}, bf16[1024,512]{1,0:T(8,128)(2,1)}) custom-call(bf16[1024,1536]{1,0:T(8,128)(2,1)} %convolution_convert_fusion.q_ref.k_ref.v_ref, bf16[1024,1536]{1,0:T(8,128)(2,1)} %convolution_convert_fusion.q_ref.k_ref.v_ref, ...), custom_call_target="tpu_custom_call" | custom-call | flops 16106127360 | bytes 8388608 | tf_op jit(solution)/shard_map/pallas_call | solution.py:163
  124.9 8.3 %shard_map.347 = bf16[2,3200,256]{2,1,0:T(8,128)(2,1)} custom-call(bf16[1024,3200]{1,0:T(8,128)(2,1)} %get-tuple-element.70.left_ref, bf16[1024,512]{1,0:T(8,128)(2,1)} %get-tuple-element.71.right_ref), custom_call_target="tpu_custom_call" | custom-call | flops 3355443200 | bytes 10878976 | tf_op jit(solution)/shard_map/pallas_call | solution.py:320
  133.4 9.9 %shard_map.346 = bf16[2,256,3200]{2,1,0:T(8,128)(2,1)} custom-call(bf16[1024,512]{1,0:T(8,128)(2,1)} %get-tuple-element.68.left_ref, bf16[1024,3200]{1,0:T(8,128)(2,1)} %get-tuple-element.69.right_ref), custom_call_target="tpu_custom_call" | custom-call | flops 3355443200 | bytes 10878976 | tf_op jit(solution)/shard_map/pallas_call | solution.py:299
  143.2 5.3 %shard_map.350 = bf16[2,256,3200]{2,1,0:T(8,128)(2,1)} custom-call(bf16[128,512]{1,0:T(8,128)(2,1)} %get-tuple-element.82.left_ref, bf16[128,3200]{1,0:T(8,128)(2,1)} %get-tuple-element.83.right_ref), custom_call_target="tpu_custom_call" | custom-call | flops 419430400 | bytes 4227072 | tf_op jit(solution)/shard_map/pallas_call | solution.py:299
  148.6 4.8 %constant_dynamic-slice_fusion = (bf16[1,256,3200]{2,1,0:T(8,128)(2,1)}, bf16[1,256,3200]{2,1,0:T(8,128)(2,1)}, bf16[1,256,3200]{2,1,0:T(8,128)(2,1)}, bf16[1,256,3200]{2,1,0:T(8,128)(2,1)}) fusion(bf16[2,256,3200]{2,1,0:T(8,128)(2,1)} %shard_map.350, s32[]{:T(128)S(6)} %select_n.129, s32[]{:T(128)S(6)} %select_n.134, bf16[2,256,3200]{2,1,0:T(8,128)(2,1)S(1)} %copy-done.8), kind=kLoop, calls=%fused_computation.87 | loop fusion | bytes 13107208 | tf_op jit(solution)/shard_map/jit(dynamic_index_in_dim)/dynamic_slice | solution.py:613
  153.4 5.3 %shard_map.351 = bf16[2,3200,256]{2,1,0:T(8,128)(2,1)} custom-call(bf16[128,3200]{1,0:T(8,128)(2,1)} %get-tuple-element.84.left_ref, bf16[128,512]{1,0:T(8,128)(2,1)} %get-tuple-element.85.right_ref), custom_call_target="tpu_custom_call" | custom-call | flops 419430400 | bytes 4227072 | tf_op jit(solution)/shard_map/pallas_call | solution.py:320
  158.7 4.4 %constant_dynamic-slice_fusion.5 = (bf16[1,3200,256]{2,1,0:T(8,128)(2,1)}, bf16[1,3200,256]{2,1,0:T(8,128)(2,1)}, bf16[1,3200,256]{2,1,0:T(8,128)(2,1)}, bf16[1,3200,256]{2,1,0:T(8,128)(2,1)S(1)}) fusion(bf16[2,3200,256]{2,1,0:T(8,128)(2,1)S(1)} %copy-done.7, s32[]{:T(128)S(6)} %select_n.129, s32[]{:T(128)S(6)} %select_n.134, ...), kind=kLoop, calls=%fused_computation.92 | loop fusion | bytes 13107208 | tf_op jit(solution)/shard_map/jit(dynamic_index_in_dim)/dynamic_slice | solution.py:613
  164.4 5.3 %shard_map.344 = bf16[2,256,1536]{2,1,0:T(8,128)(2,1)} custom-call(bf16[1024,512]{1,0:T(8,128)(2,1)} %copy-done.10, bf16[1024,1536]{1,0:T(8,128)(2,1)} %constant_dynamic-update-slice_fusion.right_ref), custom_call_target="tpu_custom_call" | custom-call | flops 1610612736 | bytes 5767168 | tf_op jit(solution)/shard_map/pallas_call | solution.py:299
  189.6 5.1 %collective-permute-done.27 = bf16[208,512]{1,0:T(8,128)(2,1)S(1)} collective-permute-done((bf16[208,512]{1,0:T(8,128)(2,1)S(1)}, bf16[208,512]{1,0:T(8,128)(2,1)S(1)}, u32[]{:S(2)}, u32[]{:S(2)}) %collective-permute-start.27) | collective-permute-done | bytes 213024 | tf_op jit(solution)/shard_map/ppermute | solution.py:582
  204.7 4.8 %collective-permute-done.29 = bf16[208,512]{1,0:T(8,128)(2,1)S(1)} collective-permute-done((bf16[208,512]{1,0:T(8,128)(2,1)S(1)}, bf16[208,512]{1,0:T(8,128)(2,1)S(1)}, u32[]{:S(2)}, u32[]{:S(2)}) %collective-permute-start.29) | collective-permute-done | bytes 213024 | tf_op jit(solution)/shard_map/ppermute | solution.py:582
  222.1 9.1 %collective-permute-done.30 = bf16[208,512]{1,0:T(8,128)(2,1)S(1)} collective-permute-done((bf16[208,512]{1,0:T(8,128)(2,1)S(1)}, bf16[208,512]{1,0:T(8,128)(2,1)S(1)}, u32[]{:S(2)}, u32[]{:S(2)}) %collective-permute-start.30) | collective-permute-done | bytes 213024 | tf_op jit(solution)/shard_map/ppermute | solution.py:582
  233.8 7.8 %shard_map.348 = (f32[128,512]{1,0:T(8,128)}, f32[512,1536]{1,0:T(8,128)}, f32[512,512]{1,0:T(8,128)}, f32[512,512]{1,0:T(8,128)}, f32[8,512]{1,0:T(8,128)}) custom-call(bf16[128,512]{1,0:T(8,128)(2,1)} %pad.20.starts_ref, bf16[512,1536]{1,0:T(8,128)(2,1)} %project_ref.3, bf16[512,512]{1,0:T(8,128)(2,1)} %combine_ref.7, bf16[512,512]{1,0:T(8,128)(2,1)} %query_ref.3, ...), custom_call_target="tpu_custom_call" | custom-call | flops 1342177280 | bytes 8388608 | tf_op jit(solution)/shard_map/pallas_call | solution.py:514
  248.4 4.5 %collective-permute-done.33 = bf16[2,2,1,1,16,1536]{5,4,3,2,1,0:T(8,128)(2,1)S(1)} collective-permute-done((bf16[2,2,1,1,16,1536]{5,4,3,2,1,0:T(8,128)(2,1)S(1)}, bf16[2,2,1,1,16,1536]{5,4,3,2,1,0:T(8,128)(2,1)S(1)}, u32[]{:S(2)}, u32[]{:S(2)}) %collective-permute-start.33) | collective-permute-done | bytes 196640 | tf_op jit(solution)/shard_map/ppermute | solution.py:582
  276.5 6.1 %collective-permute-done.5 = bf16[2,2,1,1,16,2048]{5,4,3,2,1,0:T(8,128)(2,1)S(1)} collective-permute-done((bf16[2,2,1,1,16,2048]{5,4,3,2,1,0:T(8,128)(2,1)S(1)}, bf16[2,2,1,1,16,2048]{5,4,3,2,1,0:T(8,128)(2,1)S(1)}, u32[]{:S(2)}, u32[]{:S(2)}) %collective-permute-start.5) | collective-permute-done | bytes 262176 | tf_op jit(solution)/shard_map/ppermute | solution.py:582
  287.5 31.6 %collective-permute-done.6 = bf16[1,2,1,1,16,2048]{5,4,3,2,1,0:T(8,128)(2,1)S(1)} collective-permute-done((bf16[1,2,1,1,16,2048]{5,4,3,2,1,0:T(8,128)(2,1)S(1)}, bf16[1,2,1,1,16,2048]{5,4,3,2,1,0:T(8,128)(2,1)S(1)}, u32[]{:S(2)}, u32[]{:S(2)}) %collective-permute-start.6) | collective-permute-done | bytes 131104 | tf_op jit(solution)/shard_map/ppermute | solution.py:582
  325.5 12.6 %collective-permute-done.7 = bf16[1,1,1,1,16,2048]{5,4,3,2,1,0:T(8,128)(2,1)S(1)} collective-permute-done((bf16[1,1,1,1,16,2048]{5,4,3,2,1,0:T(8,128)(2,1)S(1)}, bf16[1,1,1,1,16,2048]{5,4,3,2,1,0:T(8,128)(2,1)S(1)}, u32[]{:S(2)}, u32[]{:S(2)}) %collective-permute-start.7) | collective-permute-done | bytes 65568 | tf_op jit(solution)/shard_map/ppermute | solution.py:582
  350.6 8.7 %collective-permute-done.16 = bf16[2,2,2,1,200,256]{5,4,3,2,1,0:T(8,128)(2,1)S(1)} collective-permute-done((bf16[2,2,2,1,200,256]{5,4,3,2,1,0:T(8,128)(2,1)S(1)}, bf16[2,2,2,1,200,256]{5,4,3,2,1,0:T(8,128)(2,1)S(1)}, u32[]{:S(2)}, u32[]{:S(2)}) %collective-permute-start.16) | collective-permute-done | bytes 819232 | tf_op jit(solution)/shard_map/ppermute | solution.py:582
  364.6 12.2 %collective-permute-done.44 = bf16[2,2,2,1,200,256]{5,4,3,2,1,0:T(8,128)(2,1)S(1)} collective-permute-done((bf16[2,2,2,1,200,256]{5,4,3,2,1,0:T(8,128)(2,1)S(1)}, bf16[2,2,2,1,200,256]{5,4,3,2,1,0:T(8,128)(2,1)S(1)}, u32[]{:S(2)}, u32[]{:S(2)}) %collective-permute-start.44) | collective-permute-done | bytes 819232 | tf_op jit(solution)/shard_map/ppermute | solution.py:582
  377.1 8.5 %collective-permute-done.39 = bf16[1,2,2,1,16,3200]{5,4,3,2,1,0:T(8,128)(2,1)S(1)} collective-permute-done((bf16[1,2,2,1,16,3200]{5,4,3,2,1,0:T(8,128)(2,1)S(1)}, bf16[1,2,2,1,16,3200]{5,4,3,2,1,0:T(8,128)(2,1)S(1)}, u32[]{:S(2)}, u32[]{:S(2)}) %collective-permute-start.39) | collective-permute-done | bytes 409632 | tf_op jit(solution)/shard_map/ppermute | solution.py:582
  402.3 9.4 %collective-permute-done.12 = bf16[2,1,1,1,16,3200]{5,4,3,2,1,0:T(8,128)(2,1)S(1)} collective-permute-done((bf16[2,1,1,1,16,3200]{5,4,3,2,1,0:T(8,128)(2,1)S(1)}, bf16[2,1,1,1,16,3200]{5,4,3,2,1,0:T(8,128)(2,1)S(1)}, u32[]{:S(2)}, u32[]{:S(2)}) %collective-permute-start.12) | collective-permute-done | bytes 204832 | tf_op jit(solution)/shard_map/ppermute | solution.py:582
  (262 shorter events, 164.9 us)
Async XLA Ops:
  44.2 165.4 %collective-permute-start = (bf16[1,1024,512]{2,1,0:T(8,128)(2,1)}, bf16[1,1024,512]{2,1,0:T(8,128)(2,1)}, u32[]{:S(2)}, u32[]{:S(2)}) collective-permute-start(bf16[1,1024,512]{2,1,0:T(8,128)(2,1)} %bitcast.74), channel_id=1, source_target_pairs={{0,16},{16,0},{1,17},{17,1},{2,18},{18,2},{3,19},{19,3},{4,20},{20... | collective-permute-start | bytes 3145736 | tf_op jit(solution)/shard_map/ppermute | solution.py:582
  70.7 111.8 %collective-permute-start.26 = (bf16[208,512]{1,0:T(8,128)(2,1)}, bf16[208,512]{1,0:T(8,128)(2,1)}, u32[]{:S(2)}, u32[]{:S(2)}) collective-permute-start(bf16[208,512]{1,0:T(8,128)(2,1)} %pad_maximum_fusion.1), channel_id=1, source_target_pairs={{0,1},{1,0},{2,3},{3,2},{4,5},{5,4},{6,7},{7,6},{8,9},{9,8},{10,11... | collective-permute-start | bytes 638984 | tf_op jit(solution)/shard_map/ppermute | solution.py:582
  76.8 124.3 %collective-permute-start.31 = (bf16[2,2,2,2,16,1536]{5,4,3,2,1,0:T(8,128)(2,1)}, bf16[2,2,2,2,16,1536]{5,4,3,2,1,0:T(8,128)(2,1)}, u32[]{:S(2)}, u32[]{:S(2)}) collective-permute-start(bf16[2,2,2,2,16,1536]{5,4,3,2,1,0:T(8,128)(2,1)} %bitcast.21), channel_id=1, source_target_pairs={{0,1},{1,0},{2,3},{3,2},{4,5},{5,4},{6,7},{7,6},{8,9},{9,8},{10,11... | collective-permute-start | bytes 2359304 | tf_op jit(solution)/shard_map/ppermute | solution.py:582
  97.7 66.6 %collective-permute-start.21 = (f32[22,512]{1,0:T(8,128)S(1)}, f32[22,512]{1,0:T(8,128)S(1)}, u32[]{:S(2)}, u32[]{:S(2)}) collective-permute-start(f32[22,512]{1,0:T(8,128)S(1)} %pad_maximum_fusion.2), channel_id=1, source_target_pairs={{0,1},{1,0},{2,3},{3,2},{4,5},{5,4},{6,7},{7,6},{8,9},{9,8},{10,11... | collective-permute-start | bytes 135176 | tf_op jit(solution)/shard_map/ppermute | solution.py:582
  97.8 115.5 %collective-permute-start.1 = (bf16[1,1024,512]{2,1,0:T(8,128)(2,1)}, bf16[1,1024,512]{2,1,0:T(8,128)(2,1)}, u32[]{:S(2)}, u32[]{:S(2)}) collective-permute-start(bf16[1,1024,512]{2,1,0:T(8,128)(2,1)} %bitcast.84), channel_id=1, source_target_pairs={{0,16},{1,17},{2,18},{3,19},{4,20},{5,21},{6,22},{7,23},{8,24},{9,... | collective-permute-start | bytes 3145736 | tf_op jit(solution)/shard_map/ppermute | solution.py:690
  181.7 36.0 %collective-permute-start.3 = (bf16[2,2,2,2,16,2048]{5,4,3,2,1,0:T(8,128)(2,1)}, bf16[2,2,2,2,16,2048]{5,4,3,2,1,0:T(8,128)(2,1)S(1)}, u32[]{:S(2)}, u32[]{:S(2)}) collective-permute-start(bf16[2,2,2,2,16,2048]{5,4,3,2,1,0:T(8,128)(2,1)} %bitcast.83), channel_id=1, source_target_pairs={{0,1},{1,0},{2,3},{3,2},{4,5},{5,4},{6,7},{7,6},{8,9},{9,8},{10,11... | collective-permute-start | bytes 3145736 | tf_op jit(solution)/shard_map/ppermute | solution.py:582
  201.0 73.2 %collective-permute-start.37 = (bf16[2,2,2,2,16,3200]{5,4,3,2,1,0:T(8,128)(2,1)}, bf16[2,2,2,2,16,3200]{5,4,3,2,1,0:T(8,128)(2,1)}, u32[]{:S(2)}, u32[]{:S(2)}) collective-permute-start(bf16[2,2,2,2,16,3200]{5,4,3,2,1,0:T(8,128)(2,1)} %bitcast.24), channel_id=1, source_target_pairs={{0,1},{1,0},{2,3},{3,2},{4,5},{5,4},{6,7},{7,6},{8,9},{9,8},{10,11... | collective-permute-start | bytes 4915208 | tf_op jit(solution)/shard_map/ppermute | solution.py:582
  209.5 76.5 %collective-permute-start.9 = (bf16[2,2,2,2,16,3200]{5,4,3,2,1,0:T(8,128)(2,1)}, bf16[2,2,2,2,16,3200]{5,4,3,2,1,0:T(8,128)(2,1)}, u32[]{:S(2)}, u32[]{:S(2)}) collective-permute-start(bf16[2,2,2,2,16,3200]{5,4,3,2,1,0:T(8,128)(2,1)} %bitcast.11), channel_id=1, source_target_pairs={{0,1},{1,0},{2,3},{3,2},{4,5},{5,4},{6,7},{7,6},{8,9},{9,8},{10,11... | collective-permute-start | bytes 4915208 | tf_op jit(solution)/shard_map/ppermute | solution.py:582
  209.6 111.0 %collective-permute-start.15 = (bf16[2,2,2,2,200,256]{5,4,3,2,1,0:T(8,128)(2,1)}, bf16[2,2,2,2,200,256]{5,4,3,2,1,0:T(8,128)(2,1)}, u32[]{:S(2)}, u32[]{:S(2)}) collective-permute-start(bf16[2,2,2,2,200,256]{5,4,3,2,1,0:T(8,128)(2,1)} %bitcast.14), channel_id=1, source_target_pairs={{0,1},{1,0},{2,3},{3,2},{4,5},{5,4},{6,7},{7,6},{8,9},{9,8},{10,11... | collective-permute-start | bytes 4915208 | tf_op jit(solution)/shard_map/ppermute | solution.py:582
  213.2 32.5 %collective-permute-start.32 = (bf16[2,2,2,1,16,1536]{5,4,3,2,1,0:T(8,128)(2,1)S(1)}, bf16[2,2,2,1,16,1536]{5,4,3,2,1,0:T(8,128)(2,1)S(1)}, u32[]{:S(2)}, u32[]{:S(2)}) collective-permute-start(bf16[2,2,2,1,16,1536]{5,4,3,2,1,0:T(8,128)(2,1)S(1)} %add_convert_fusion.10), channel_id=1, source_target_pairs={{0,2},{2,0},{4,6},{6,4},{8,10},{10,8},{12,14},{14,12},{1,3},{3,1},... | collective-permute-start | bytes 1179656 | tf_op jit(solution)/shard_map/ppermute | solution.py:582
  231.2 37.6 %collective-permute-start.4 = (bf16[2,2,2,1,16,2048]{5,4,3,2,1,0:T(8,128)(2,1)}, bf16[2,2,2,1,16,2048]{5,4,3,2,1,0:T(8,128)(2,1)}, u32[]{:S(2)}, u32[]{:S(2)}) collective-permute-start(bf16[2,2,2,1,16,2048]{5,4,3,2,1,0:T(8,128)(2,1)} %add_convert_fusion.5), channel_id=1, source_target_pairs={{0,2},{2,0},{4,6},{6,4},{8,10},{10,8},{12,14},{14,12},{1,3},{3,1},... | collective-permute-start | bytes 1572872 | tf_op jit(solution)/shard_map/ppermute | solution.py:582
  267.8 72.2 %collective-permute-start.43 = (bf16[2,2,2,2,200,256]{5,4,3,2,1,0:T(8,128)(2,1)}, bf16[2,2,2,2,200,256]{5,4,3,2,1,0:T(8,128)(2,1)S(1)}, u32[]{:S(2)}, u32[]{:S(2)}) collective-permute-start(bf16[2,2,2,2,200,256]{5,4,3,2,1,0:T(8,128)(2,1)} %bitcast.82), channel_id=1, source_target_pairs={{0,1},{1,0},{2,3},{3,2},{4,5},{5,4},{6,7},{7,6},{8,9},{9,8},{10,11... | collective-permute-start | bytes 4915208 | tf_op jit(solution)/shard_map/ppermute | solution.py:582
  271.4 71.0 %collective-permute-start.2 = (bf16[1,1024,512]{2,1,0:T(8,128)(2,1)}, bf16[1,1024,512]{2,1,0:T(8,128)(2,1)S(1)}, u32[]{:S(2)}, u32[]{:S(2)}) collective-permute-start(bf16[1,1024,512]{2,1,0:T(8,128)(2,1)} %get-tuple-element.158), channel_id=1, source_target_pairs={{16,0},{17,1},{18,2},{19,3},{20,4},{21,5},{22,6},{23,7},{24,8},{25... | collective-permute-start | bytes 3145736 | tf_op jit(solution)/shard_map/ppermute | solution.py:691
  282.6 62.9 %collective-permute-start.38 = (bf16[1,2,2,2,16,3200]{5,4,3,2,1,0:T(8,128)(2,1)S(1)}, bf16[1,2,2,2,16,3200]{5,4,3,2,1,0:T(8,128)(2,1)S(1)}, u32[]{:S(2)}, u32[]{:S(2)}) collective-permute-start(bf16[1,2,2,2,16,3200]{5,4,3,2,1,0:T(8,128)(2,1)S(1)} %add_convert_fusion.2), channel_id=1, source_target_pairs={{0,16},{16,0},{1,17},{17,1},{2,18},{18,2},{3,19},{19,3},{4,20},{20... | collective-permute-start | bytes 2457608 | tf_op jit(solution)/shard_map/ppermute | solution.py:582
  286.0 33.0 %collective-permute-start.6 = (bf16[1,2,1,1,16,2048]{5,4,3,2,1,0:T(8,128)(2,1)S(1)}, bf16[1,2,1,1,16,2048]{5,4,3,2,1,0:T(8,128)(2,1)S(1)}, u32[]{:S(2)}, u32[]{:S(2)}) collective-permute-start(bf16[1,2,1,1,16,2048]{5,4,3,2,1,0:T(8,128)(2,1)S(1)} %add_convert_fusion.21), channel_id=1, source_target_pairs={{0,16},{16,0},{1,17},{17,1},{2,18},{18,2},{3,19},{19,3},{4,20},{20... | collective-permute-start | bytes 393224 | tf_op jit(solution)/shard_map/ppermute | solution.py:582
  319.0 29.3 %collective-permute-start.10 = (bf16[2,2,1,2,16,3200]{5,4,3,2,1,0:T(8,128)(2,1)S(1)}, bf16[2,2,1,2,16,3200]{5,4,3,2,1,0:T(8,128)(2,1)S(1)}, u32[]{:S(2)}, u32[]{:S(2)}) collective-permute-start(bf16[2,2,1,2,16,3200]{5,4,3,2,1,0:T(8,128)(2,1)S(1)} %add_convert_fusion.4), channel_id=1, source_target_pairs={{0,4},{2,6},{4,0},{6,2},{8,12},{10,14},{12,8},{14,10},{1,5},{3,7},... | collective-permute-start | bytes 2457608 | tf_op jit(solution)/shard_map/ppermute | solution.py:582
  338.1 21.2 %collective-permute-start.16 = (bf16[2,2,2,1,200,256]{5,4,3,2,1,0:T(8,128)(2,1)S(1)}, bf16[2,2,2,1,200,256]{5,4,3,2,1,0:T(8,128)(2,1)S(1)}, u32[]{:S(2)}, u32[]{:S(2)}) collective-permute-start(bf16[2,2,2,1,200,256]{5,4,3,2,1,0:T(8,128)(2,1)S(1)} %add_convert_fusion.3), channel_id=1, source_target_pairs={{0,2},{2,0},{4,6},{6,4},{8,10},{10,8},{12,14},{14,12},{1,3},{3,1},... | collective-permute-start | bytes 2457608 | tf_op jit(solution)/shard_map/ppermute | solution.py:582
  341.3 35.5 %collective-permute-start.44 = (bf16[2,2,2,1,200,256]{5,4,3,2,1,0:T(8,128)(2,1)S(1)}, bf16[2,2,2,1,200,256]{5,4,3,2,1,0:T(8,128)(2,1)S(1)}, u32[]{:S(2)}, u32[]{:S(2)}) collective-permute-start(bf16[2,2,2,1,200,256]{5,4,3,2,1,0:T(8,128)(2,1)S(1)} %add_convert_fusion.1), channel_id=1, source_target_pairs={{0,2},{2,0},{4,6},{6,4},{8,10},{10,8},{12,14},{14,12},{1,3},{3,1},... | collective-permute-start | bytes 2457608 | tf_op jit(solution)/shard_map/ppermute | solution.py:582
  347.3 38.3 %collective-permute-start.39 = (bf16[1,2,2,1,16,3200]{5,4,3,2,1,0:T(8,128)(2,1)S(1)}, bf16[1,2,2,1,16,3200]{5,4,3,2,1,0:T(8,128)(2,1)S(1)}, u32[]{:S(2)}, u32[]{:S(2)}) collective-permute-start(bf16[1,2,2,1,16,3200]{5,4,3,2,1,0:T(8,128)(2,1)S(1)} %add_convert_fusion.7), channel_id=1, source_target_pairs={{0,2},{2,0},{4,6},{6,4},{8,10},{10,8},{12,14},{14,12},{1,3},{3,1},... | collective-permute-start | bytes 1228808 | tf_op jit(solution)/shard_map/ppermute | solution.py:582
  349.5 42.3 %collective-permute-start.11 = (bf16[2,2,1,1,16,3200]{5,4,3,2,1,0:T(8,128)(2,1)S(1)}, bf16[2,2,1,1,16,3200]{5,4,3,2,1,0:T(8,128)(2,1)S(1)}, u32[]{:S(2)}, u32[]{:S(2)}) collective-permute-start(bf16[2,2,1,1,16,3200]{5,4,3,2,1,0:T(8,128)(2,1)S(1)} %add_convert_fusion.9), channel_id=1, source_target_pairs={{0,2},{2,0},{4,6},{6,4},{8,10},{10,8},{12,14},{14,12},{1,3},{3,1},... | collective-permute-start | bytes 1228808 | tf_op jit(solution)/shard_map/ppermute | solution.py:582
  360.5 35.5 %collective-permute-start.17 = (bf16[2,2,1,1,200,256]{5,4,3,2,1,0:T(8,128)(2,1)S(1)}, bf16[2,2,1,1,200,256]{5,4,3,2,1,0:T(8,128)(2,1)S(1)}, u32[]{:S(2)}, u32[]{:S(2)}) collective-permute-start(bf16[2,2,1,1,200,256]{5,4,3,2,1,0:T(8,128)(2,1)S(1)} %add_convert_fusion.8), channel_id=1, source_target_pairs={{0,4},{2,6},{4,0},{6,2},{8,12},{10,14},{12,8},{14,10},{1,5},{3,7},... | collective-permute-start | bytes 1228808 | tf_op jit(solution)/shard_map/ppermute | solution.py:582
  377.0 20.1 %collective-permute-start.45 = (bf16[1,2,2,1,200,256]{5,4,3,2,1,0:T(8,128)(2,1)S(1)}, bf16[1,2,2,1,200,256]{5,4,3,2,1,0:T(8,128)(2,1)S(1)}, u32[]{:S(2)}, u32[]{:S(2)}) collective-permute-start(bf16[1,2,2,1,200,256]{5,4,3,2,1,0:T(8,128)(2,1)S(1)} %add_convert_fusion.6), channel_id=1, source_target_pairs={{0,16},{16,0},{1,17},{17,1},{2,18},{18,2},{3,19},{19,3},{4,20},{20... | collective-permute-start | bytes 1228808 | tf_op jit(solution)/shard_map/ppermute | solution.py:582
  397.0 19.0 %collective-permute-start.18 = (bf16[2,1,1,1,200,256]{5,4,3,2,1,0:T(8,128)(2,1)S(1)}, bf16[2,1,1,1,200,256]{5,4,3,2,1,0:T(8,128)(2,1)S(1)}, u32[]{:S(2)}, u32[]{:S(2)}) collective-permute-start(bf16[2,1,1,1,200,256]{5,4,3,2,1,0:T(8,128)(2,1)S(1)} %add_convert_fusion.18), channel_id=1, source_target_pairs={{0,8},{2,10},{4,12},{6,14},{8,0},{10,2},{12,4},{14,6},{1,9},{3,11}... | collective-permute-start | bytes 614408 | tf_op jit(solution)/shard_map/ppermute | solution.py:582
  397.2 19.9 %collective-permute-start.46 = (bf16[1,2,1,1,200,256]{5,4,3,2,1,0:T(8,128)(2,1)S(1)}, bf16[1,2,1,1,200,256]{5,4,3,2,1,0:T(8,128)(2,1)S(1)}, u32[]{:S(2)}, u32[]{:S(2)}) collective-permute-start(bf16[1,2,1,1,200,256]{5,4,3,2,1,0:T(8,128)(2,1)S(1)} %add_convert_fusion.16), channel_id=1, source_target_pairs={{0,4},{2,6},{4,0},{6,2},{8,12},{10,14},{12,8},{14,10},{1,5},{3,7},... | collective-permute-start | bytes 614408 | tf_op jit(solution)/shard_map/ppermute | solution.py:582
  (62 other events, 553.6 us)
